TPU v7x, 32 devices: a whole 2x2x4 slice. The times are simulated.
32 devices in a mesh: tok: 4 (over z), blk: 8 (over y, x, core).
Axes of the slice: x: 2, y: 2, z: 4, core: 2. Of those that a mesh axis runs over, the one named last changes fastest.
Arguments:
- student_in: bfloat16 [7168, 8192], P('tok', 'blk'), may hold values from -6 to 6
- teacher_out: bfloat16 [7168, 8192], P('tok', 'blk'), may hold values from -6 to 6
- w_first: bfloat16 [64, 128, 512], P('blk'), may hold values from -0.5 to 0.5
- w_second: bfloat16 [256, 128, 128], P('blk'), may hold values from -0.5 to 0.5
- w_third: bfloat16 [256, 128, 32], P('blk'), may hold values from -0.5 to 0.5
- w_fourth: bfloat16 [32, 256, 256], P('blk'), may hold values from -0.375 to 0.375
Outputs:
- grad_first: float32 [64, 128, 512], P('blk')
- grad_second: float32 [256, 128, 128], P('blk')
- grad_third: float32 [256, 128, 32], P('blk')
- grad_fourth: float32 [32, 256, 256], P('blk')
All inputs are finite; a program needn't handle non-finite values.
Results may differ from a plain program's by a relative error of at most 0.004.
Values may be sent and summed in bfloat16 or wider, within the bound.
No kernel may reach another device: no remote copies, remote signals or barrier semaphores. Data moves between devices by JAX's collectives and lax.ppermute only.
A program may use at most 256 MiB of HBM per device.

v0:
```python
import jax
import jax.numpy as jnp
from jax import lax
from jax.sharding import PartitionSpec as P


def gelu_slope(value):
    cdf_part = 0.5 * (1.0 + jax.scipy.special.erf(value * 0.7071067811865476))
    return cdf_part + value * jnp.exp(-0.5 * value * value) * 0.3989422804014327


def shards(student_in, teacher_out, w_first, w_second, w_third, w_fourth):
    f32 = jnp.float32
    bf16 = jnp.bfloat16
    blk_count = lax.axis_size("blk")
    tok_rows = student_in.shape[0]
    blk_width = w_first.shape[1]
    first_local = w_first.shape[0]
    n_first = first_local * blk_count
    first_cols_count = w_first.shape[2]
    second_local = w_second.shape[0]
    n_second = second_local * blk_count
    spread = first_cols_count // n_second
    last_local = w_fourth.shape[0]
    out_width = w_fourth.shape[2]
    factor = 1.0 / float(tok_rows * lax.axis_size("tok")) ** 0.5
    local_in = student_in.reshape(tok_rows, first_local, blk_width)
    first_out = jnp.einsum("tai,air->art", local_in, w_first, preferred_element_type=f32).astype(
        bf16
    )
    first_view = first_out.reshape(first_local, spread, n_second, tok_rows)
    mixed = lax.all_to_all(first_view, "blk", split_axis=2, concat_axis=0, tiled=True)
    second_view = w_second.reshape(second_local, n_first, spread, blk_width)
    pre_act = jnp.einsum("axgt,gaxo->got", mixed, second_view, preferred_element_type=f32)
    hidden = jax.nn.gelu(pre_act, approximate=False).astype(bf16)
    third_out = jnp.einsum("got,goe->get", hidden, w_third, preferred_element_type=f32).astype(bf16)
    third_recv = lax.all_to_all(third_out, "blk", split_axis=1, concat_axis=0, tiled=True)
    student = jnp.einsum("get,ego->teo", third_recv, w_fourth, preferred_element_type=f32)
    target = teacher_out.reshape(tok_rows, last_local, out_width).astype(f32)
    slope_out = ((student - target) * factor).astype(bf16)
    grad_four = jnp.einsum("get,teo->ego", third_recv, slope_out, preferred_element_type=f32)
    back_third = jnp.einsum("teo,ego->get", slope_out, w_fourth, preferred_element_type=f32).astype(
        bf16
    )
    slope_third = lax.all_to_all(back_third, "blk", split_axis=0, concat_axis=1, tiled=True)
    grad_three = jnp.einsum("got,get->goe", hidden, slope_third, preferred_element_type=f32)
    back_hidden = jnp.einsum("get,goe->got", slope_third, w_third, preferred_element_type=f32)
    slope_pre = (back_hidden * gelu_slope(pre_act)).astype(bf16)
    grad_two = jnp.einsum("axgt,got->gaxo", mixed, slope_pre, preferred_element_type=f32).reshape(
        second_local, blk_width, blk_width
    )
    slope_mixed = jnp.einsum(
        "got,gaxo->axgt", slope_pre, second_view, preferred_element_type=f32
    ).astype(bf16)
    slope_first = lax.all_to_all(slope_mixed, "blk", split_axis=0, concat_axis=2, tiled=True)
    grad_part = jnp.einsum("tai,axgt->aixg", local_in, slope_first, preferred_element_type=f32)
    grad_part, grad_two, grad_three, grad_four = lax.psum(
        (grad_part, grad_two, grad_three, grad_four), "tok"
    )
    grad_one = grad_part
    grad_one = grad_one.reshape(first_local, blk_width, first_cols_count)
    return (grad_one, grad_two, grad_three, grad_four)


def solution(mesh):
    placed = (
        P("tok", "blk"),
        P("tok", "blk"),
        P("blk", None, None),
        P("blk", None, None),
        P("blk", None, None),
        P("blk", None, None),
    )
    return jax.shard_map(
        shards,
        mesh=mesh,
        in_specs=placed,
        out_specs=(
            P("blk", None, None),
            P("blk", None, None),
            P("blk", None, None),
            P("blk", None, None),
        ),
        check_vma=False,
    )
```

profile of v0, /device:TPU:0, one launch (start us, length us, event | category | flops | bytes accessed | tf_op | source)
XLA Modules:
  0.0 896.0 jit_solution(10928908848251143513)
XLA Ops:
  7.2 11.7 %convolution_convert_fusion = bf16[8,512,1792]{2,1,0:T(8,128)(2,1)} fusion(bf16[8,128,512]{2,1,0:T(8,128)(2,1)} %param.8, bf16[1792,1024]{1,0:T(8,128)(2,1)} %param.6), kind=kOutput, calls=%fused_computation.42 | convolution fusion | flops 1886388224 | bytes 19398656 | tf_op jit(solution)/shard_map/tai,air->art/dot_general | solution.py:28
  18.8 26.6 %copy.70 = bf16[8,2,256,1792]{3,1,0,2:T(2,128)(2,1)S(1)} copy(bf16[8,2,256,1792]{3,2,1,0:T(8,128)(2,1)} %bitcast.132) | data formatting | bytes 29360128 | tf_op jit(solution)/shard_map/reshape | solution.py:31
  45.5 166.7 %all_to_all.72 = bf16[8,2,256,1792]{3,1,0,2:T(2,128)(2,1)} all-to-all(bf16[8,2,256,1792]{3,1,0,2:T(2,128)(2,1)S(1)} %copy.70), channel_id=1, replica_groups=mesh['tok'=4,'blk'=8] {'blk'}, dimensions={2} | all-to-all | bytes 29360128 | tf_op jit(solution)/shard_map/all_to_all | solution.py:32
  212.2 70.5 %fusion.2 = (bf16[32,128,1792]{1,2,0:T(8,128)(2,1)S(1)}, f32[32,1792,128,1]{2,1,3,0:T(8,128)}) fusion(bf16[32,64,2,128]{3,2,1,0:T(2,128)(2,1)S(1)} %bitcast.128, bf16[8,2,8,32,1792]{4,1,0,3,2:T(2,128)(2,1)} %bitcast.134), kind=kOutput, calls=%fused_computation.4 | convolution fusion | flops 2356150272 | bytes 59768832 | tf_op jit(solution)/shard_map/axgt,gaxo->got/dot_general | solution.py:34
  282.7 5.1 copy-done.1
  287.8 6.1 fusion.40
  302.7 5.9 copy.77
  308.6 6.2 copy.78
  314.8 31.4 %all-to-all-done.1 = bf16[32,32,1792]{2,0,1:T(8,128)(2,1)} async-done(((bf16[32,32,1792]{2,0,1:T(8,128)(2,1)}), bf16[32,32,1792]{2,0,1:T(8,128)(2,1)}, u32[]{:S(2)}, u32[]{:S(2)}) %all-to-all-start.1) | async-done | bytes 3670048 | tf_op jit(solution)/shard_map/all_to_all | solution.py:37
  360.3 6.9 copy.79
  367.1 47.0 %all_to_all.73 = bf16[256,4,1792]{2,1,0:T(4,128)(2,1)S(1)} all-to-all(bf16[256,4,1792]{2,1,0:T(4,128)(2,1)} %copy.79), channel_id=1, replica_groups=mesh['tok'=4,'blk'=8] {'blk'}, dimensions={0} | all-to-all | bytes 7340032 | tf_op jit(solution)/shard_map/all_to_all | solution.py:45
  419.2 6.9 all_to_all.63
  426.1 21.6 %fusion.8 = bf16[32,128,1792]{1,2,0:T(8,128)(2,1)} fusion(f32[32,1792,128,1]{2,1,3,0:T(8,128)} %get-tuple-element.21, bf16[32,32,1792]{2,1,0:T(8,128)(2,1)} %all_to_all.63, bf16[32,128,32]{1,2,0:T(8,128)(2,1)S(1)} %copy-done.6), kind=kOutput, calls=%fused_computation.10 | convolution fusion | flops 543162368 | bytes 47972352 | tf_op jit(solution)/shard_map/get,goe->got/dot_general | solution.py:47
  447.7 10.4 %convert_bitcast_fusion = bf16[64,2,32,1792]{3,0,1,2:T(8,128)(2,1)} fusion(bf16[32,128,1792]{1,2,0:T(8,128)(2,1)} %fusion.8, bf16[32,64,2,128]{3,2,1,0:T(2,128)(2,1)S(1)} %bitcast.129), kind=kOutput, calls=%fused_computation.41 | convolution fusion | flops 1886388224 | bytes 30408704 | tf_op jit(solution)/shard_map/got,gaxo->axgt/dot_general | solution.py:52
  458.1 21.8 %copy.84 = bf16[64,2,32,1792]{3,1,2,0:T(2,128)(2,1)} copy(bf16[64,2,32,1792]{3,0,1,2:T(8,128)(2,1)} %convert_bitcast_fusion) | data formatting | bytes 29360128 | tf_op jit(solution)/shard_map/convert_element_type | solution.py:54
  479.9 5.6 all-to-all-start.3
  485.8 5.0 copy.107
  490.8 5.4 fusion.44
  496.2 12.9 %fusion.23 = f32[32,64,2,128]{3,1,2,0:T(8,128)} fusion(bf16[32,128,1792]{1,2,0:T(8,128)(2,1)} %fusion.8, bf16[8,2,8,32,1792]{4,1,0,3,2:T(2,128)(2,1)} %bitcast.135), kind=kOutput, calls=%fused_computation.34 | convolution fusion | flops 1879048192 | bytes 31457280 | tf_op jit(solution)/shard_map/axgt,got->gaxo/dot_general | solution.py:49
  513.3 5.2 fusion.45
  518.5 128.5 %all-to-all-done.3 = bf16[64,2,32,1792]{3,1,2,0:T(2,128)(2,1)} async-done(((bf16[64,2,32,1792]{3,1,2,0:T(2,128)(2,1)}), bf16[64,2,32,1792]{3,1,2,0:T(2,128)(2,1)}, u32[]{:S(2)}, u32[]{:S(2)}) %all-to-all-start.3) | async-done | bytes 14680096 | tf_op jit(solution)/shard_map/all_to_all | solution.py:55
  647.0 14.8 %copy.85 = bf16[8,8,2,32,1792]{4,3,0,2,1:T(8,128)(2,1)} copy(bf16[8,8,2,32,1792]{4,2,3,1,0:T(2,128)(2,1)} %bitcast.21) | data formatting | bytes 29360128 | tf_op jit(solution)/shard_map/all_to_all | solution.py:55
  661.8 7.3 fusion.38
  670.9 206.5 %all-reduce.3.cloned.1.call-done = (f32[8,128,512]{2,1,0:T(8,128)}, f32[32,128,128]{2,0,1:T(8,128)}, f32[32,128,32]{1,2,0:T(8,128)}, f32[4,256,256]{2,1,0:T(8,128)}) async-done(((f32[8,128,512]{2,1,0:T(8,128)}, f32[32,128,128]{2,0,1:T(8,128)}, f32[32,128,32]{1,2,0:T(8,128)}, f32[4,256,256]{2,1,0:T(8,128)}), (f32[8,128,512]{2,1,0:T(8,128)}, f32[32,128,128]{2,0,1:T(8,128)}, f32[32,128,32]{1,2,0:T(8,128)}, ...) | async-done | bytes 5767184 | tf_op jit(solution)/shard_map/psum | solution.py:57
  (37 shorter events, 45.5 us)
Async XLA Ops:
  7.2 205.0 %copy-start = (bf16[32,128,128]{2,1,0:T(8,128)(2,1)S(1)}, bf16[32,128,128]{2,1,0:T(8,128)(2,1)}, u32[]{:S(2)}) copy-start(bf16[32,128,128]{2,1,0:T(8,128)(2,1)} %param.9) | copy-start | bytes 3145732
  282.7 5.1 copy-start.1
  297.8 52.6 %copy-start.5 = (bf16[4,256,256]{2,1,0:T(8,128)(2,1)S(1)}, bf16[4,256,256]{2,1,0:T(8,128)(2,1)}, u32[]{:S(2)}) copy-start(bf16[4,256,256]{2,1,0:T(8,128)(2,1)} %param.11) | copy-start | bytes 1572868
  297.8 48.4 %all-to-all-start.1 = ((bf16[32,32,1792]{2,0,1:T(8,128)(2,1)}), bf16[32,32,1792]{2,0,1:T(8,128)(2,1)}, u32[]{:S(2)}, u32[]{:S(2)}) async-start(bf16[32,32,1792]{2,0,1:T(8,128)(2,1)} %copy.74), calls=%async_computation.1 | async-start | bytes 7340032 | tf_op jit(solution)/shard_map/all_to_all | solution.py:37
  348.6 1.9 copy-start.2
  350.4 75.7 %copy-start.6 = (bf16[32,128,32]{1,2,0:T(8,128)(2,1)S(1)}, bf16[32,128,32]{1,2,0:T(8,128)(2,1)}, u32[]{:S(2)}) copy-start(bf16[32,128,32]{1,2,0:T(8,128)(2,1)} %param.10) | copy-start | bytes 786436
  355.3 2.0 copy-start.3
  479.9 167.1 %all-to-all-start.3 = ((bf16[64,2,32,1792]{3,1,2,0:T(2,128)(2,1)}), bf16[64,2,32,1792]{3,1,2,0:T(2,128)(2,1)}, u32[]{:S(2)}, u32[]{:S(2)}) async-start(bf16[64,2,32,1792]{3,1,2,0:T(2,128)(2,1)} %copy.84), calls=%async_computation.3 | async-start | bytes 29360128 | tf_op jit(solution)/shard_map/all_to_all | solution.py:55
  485.5 391.9 %all-reduce.3.cloned.1.call-start = ((), (), s32[]{:S(2)}) async-start(), calls=%async_computation.4 | async-start | bytes 11534336 | tf_op jit(solution)/shard_map/psum | solution.py:57
  485.8 27.5 %slice-start = ((s8[14680064]{0:T(1024)(128)(4,1)}), s8[4194304]{0:T(1024)(128)(4,1)S(1)}, s32[]{:S(2)}) async-start(s8[14680064]{0:T(1024)(128)(4,1)} %bitcast.130), calls=%async_computation.5 | async-start | bytes 8388608
  490.8 22.5 %slice-start.1 = ((s8[14680064]{0:T(1024)(128)(4,1)}), s8[4194304]{0:T(1024)(128)(4,1)S(1)}, s32[]{:S(2)}) async-start(s8[14680064]{0:T(1024)(128)(4,1)} %bitcast.130), calls=%async_computation.6 | async-start | bytes 8388608
  496.2 17.1 %slice-start.2 = ((s8[14680064]{0:T(1024)(128)(4,1)}), s8[4194304]{0:T(1024)(128)(4,1)S(1)}, s32[]{:S(2)}) async-start(s8[14680064]{0:T(1024)(128)(4,1)} %bitcast.130), calls=%async_computation.7 | async-start | bytes 8388608
  496.2 17.1 %slice-start.3 = ((s8[14680064]{0:T(1024)(128)(4,1)}), s8[2097152]{0:T(1024)(128)(4,1)S(1)}, s32[]{:S(2)}) async-start(s8[14680064]{0:T(1024)(128)(4,1)} %bitcast.130), calls=%async_computation.8 | async-start | bytes 4194304
  647.0 14.8 %copy-start.4 = (bf16[224,8,8,128]{3,2,1,0:T(8,128)(2,1)S(1)}, bf16[224,8,8,128]{3,2,1,0:T(8,128)(2,1)}, u32[]{:S(2)}) copy-start(bf16[224,8,8,128]{3,2,1,0:T(8,128)(2,1)} %copy.107) | copy-start | bytes 11010052
Sparse Core Ops, SparseCore 0:
  671.0 206.3 all-reduce.2
where the time goes:
time: 902 us; the launch traced here: 896 us
  waiting for transfers between devices  366 us (41%)
  blocking collectives  214 us (24%)
  matrix products  159 us (18%)
  local copies, waits for them, and re-layouts  132 us (15%)
  between operations  14.6 us (2%)
  starting transfers between devices  10.8 us (1%)
    psum x1, waiting for transfers between devices, shards(): lax.psum((grad_part, grad_two, grad_three, grad_four), 'tok')  207 us
    all_to_all x1, blocking collectives, shards(): lax.all_to_all(first_view, 'blk', split_axis=2, concat_axis=0, tiled=True)  167 us
    all_to_all x1, waiting for transfers between devices, shards(): lax.all_to_all(slope_mixed, 'blk', split_axis=0, concat_axis=2, tiled=True)  128 us
    dot_general x1, matrix products, shards(): jnp.einsum('axgt,gaxo->got', mixed, second_view, preferred_element_type=f32)  70.5 us
    all_to_all x1, blocking collectives, shards(): lax.all_to_all(back_third, 'blk', split_axis=0, concat_axis=1, tiled=True)  47 us
    all_to_all x1, waiting for transfers between devices, shards(): lax.all_to_all(third_out, 'blk', split_axis=1, concat_axis=0, tiled=True)  31.4 us
    unnamed x28, local copies, waits for them, and re-layouts  31.3 us
    reshape x1, local copies, waits for them, and re-layouts, shards(): first_view = first_out.reshape(first_local, spread, n_second, tok_rows)  26.6 us
  transfers between devices with their start and end apart: 3, of which 3 were waited for; matrix products, arithmetic and copies ran while one was open for 5% of the time, Pallas kernels for 0%

commit v1 on v0

v1 whole, which is shorter than its diff:
```python
import functools

import jax
import jax.numpy as jnp
from jax import lax
from jax.experimental import pallas as pl
from jax.experimental.pallas import tpu as pltpu
from jax.sharding import PartitionSpec as P

F32 = jnp.float32
BF16 = jnp.bfloat16
TILE = 256
CUTS = (0, 3, 7)
PLAN = ("f0", "f1", "m0", "m1", "q0", "b0", "q1", "b1", "q2", "r0", "x0", "q3", "r1", "x1", "r2", "q4")
ROWS = 16
SUB = 8
LANES = 128
SQRT_HALF = 0.7071067811865476
INV_SQRT_2PI = 0.3989422804014327
VMEM_BYTES = 56 * 1024 * 1024


def nn(a, b):
    return jnp.dot(a, b, preferred_element_type=F32)


def nt(a, b):
    return lax.dot_general(a, b, (((1,), (1,)), ((), ())), preferred_element_type=F32)


def whole(shape):
    return pl.BlockSpec(shape, lambda t: (0,) * len(shape), pipeline_mode=pl.Buffered(1))


def tokens_last(shape):
    lead = len(shape) - 1
    return pl.BlockSpec(shape[:-1] + (TILE,), lambda t: (0,) * lead + (t,))


def piece_spec(shape, row):
    return pl.BlockSpec((TILE, shape[1]), lambda t: (t + row // TILE, 0))


def smem():
    return pl.BlockSpec(memory_space=pltpu.SMEM)


def call(body, grid, in_specs, out_specs, out_shape, scratch, flops, moved):
    return pl.pallas_call(
        body,
        grid=(grid,),
        in_specs=in_specs,
        out_specs=out_specs,
        out_shape=out_shape,
        scratch_shapes=scratch,
        compiler_params=pltpu.CompilerParams(vmem_limit_bytes=VMEM_BYTES),
        cost_estimate=pl.CostEstimate(flops=flops, bytes_accessed=moved, transcendentals=0),
    )


def forward(pieces, order, span, w1, w2_t, w3_t, n_dev):
    n_piece, rows1, in_width = w1.shape
    tok = span[1] - span[0]
    depth1 = pieces[0].shape[1]
    n_a = depth1 // in_width
    n_g, bw, fan = w2_t.shape
    spread = fan // n_piece // n_a
    n_q, third_rows, third_depth = w3_t.shape
    gq = n_g // n_q

    def body(*refs):
        x_refs = refs[:n_piece]
        order_ref, w1_ref, w2_ref, w3_ref, first_ref, third_ref, wide_ref, hid_ref = refs[n_piece:]

        @pl.when(pl.program_id(0) == 0)
        def _():
            owner = lax.broadcasted_iota(jnp.int32, (rows1, in_width), 0) // spread % n_a

            @pl.loop(0, n_piece)
            def _(p):
                rows = w1_ref[p].astype(F32)
                for a in range(n_a):
                    block = jnp.where(owner == a, rows, 0.0).astype(BF16)
                    wide_ref[p, :, a * in_width : (a + 1) * in_width] = block

        for k in range(0, n_piece, 2):
            both = []
            for j in range(2):
                part = nt(wide_ref[order_ref[k + j]], x_refs[k + j][...])
                both.append(part.reshape(n_g, SUB, TILE))
            at = pl.multiple_of(order_ref[k] * SUB, ROWS)
            first_ref[:, pl.ds(at, ROWS), :] = jnp.concatenate(both, axis=1).astype(BF16)

        @pl.loop(0, n_q, unroll=n_q)
        def _(q):
            for j in range(gq):
                pre = nn(w2_ref[q * gq + j], first_ref[q * gq + j])
                cdf = 0.5 * (1.0 + lax.erf(pre * SQRT_HALF))
                hid_ref[j * bw : (j + 1) * bw, :] = (pre * cdf).astype(BF16)
            out = nn(w3_ref[q], hid_ref[...]).astype(BF16)
            third_ref[:, pl.ds(q * ROWS, ROWS), :] = out.reshape(n_dev, ROWS, TILE)

    first_shape = (n_g, fan, tok)
    third_shape = (n_dev, n_q * ROWS, tok)
    return call(
        body,
        tok // TILE,
        [piece_spec(p.shape, span[0]) for p in pieces]
        + [smem(), whole(w1.shape), whole(w2_t.shape), whole(w3_t.shape)],
        [tokens_last(first_shape), tokens_last(third_shape)],
        [jax.ShapeDtypeStruct(first_shape, BF16), jax.ShapeDtypeStruct(third_shape, BF16)],
        [pltpu.VMEM((n_piece, rows1, depth1), BF16), pltpu.VMEM((gq * bw, TILE), BF16)],
        2 * tok * (n_piece * rows1 * depth1 + n_g * bw * fan + n_q * third_rows * third_depth),
        2 * (n_piece * depth1 * tok + w1.size + n_g * fan * tok),
    )(*pieces, order, w1, w2_t, w3_t)


def middle(third, teacher, row, w4_big, w4_big_t, factor, last_local, held_sum, last):
    n_dev, dev_rows, tok = third.shape
    rows, cols = w4_big.shape
    width = cols // last_local
    per_e = rows // last_local
    n_col = width // LANES
    sum_shape = (n_col, rows, LANES)
    grad_shape = (last_local, per_e, width) if last else sum_shape
    sums = [] if held_sum is None else [held_sum]

    def body(third_ref, teach_ref, w4_ref, w4t_ref, *refs):
        start_refs, (back_ref, grad_ref, acc_ref) = refs[: len(sums)], refs[len(sums) :]
        t = pl.program_id(0)

        @pl.when(t == 0)
        def _():
            acc_ref[...] = start_refs[0][...] if sums else jnp.zeros_like(acc_ref)

        held = third_ref[...].reshape(rows, TILE)
        student = nn(w4t_ref[...], held)
        target = teach_ref[...].astype(F32).T
        slope = ((student - target) * factor).astype(BF16)
        back = nn(w4_ref[...], slope).astype(BF16)
        back_ref[...] = back.reshape(n_dev, dev_rows, TILE)
        owner = lax.broadcasted_iota(jnp.int32, (rows, LANES), 0) % last_local
        for e in range(last_local):
            part = nt(held, slope[e * width : (e + 1) * width, :])
            for c in range(n_col):
                cols_c = part[:, c * LANES : (c + 1) * LANES]
                acc_ref[c] += jnp.where(owner == e, cols_c, 0.0)

        @pl.when(t == pl.num_programs(0) - 1)
        def _():
            if not last:
                grad_ref[...] = acc_ref[...]
                return
            for e in range(last_local):
                for c in range(n_col):
                    picked = acc_ref[c, pl.ds(e, per_e, stride=last_local), :]
                    grad_ref[e, :, c * LANES : (c + 1) * LANES] = picked

    return call(
        body,
        tok // TILE,
        [
            tokens_last(third.shape),
            pl.BlockSpec((TILE, cols), lambda t: (t + row // TILE, 0)),
            whole(w4_big.shape),
            whole(w4_big_t.shape),
        ]
        + [whole(a.shape) for a in sums],
        [tokens_last(third.shape), whole(grad_shape)],
        [jax.ShapeDtypeStruct(third.shape, BF16), jax.ShapeDtypeStruct(grad_shape, F32)],
        [pltpu.VMEM(sum_shape, F32)],
        6 * tok * rows * cols,
        2 * (3 * third.size + 2 * rows * cols),
    )(third, teacher, w4_big, w4_big_t, *sums)


def backward(turns, first, back, w2, w2_t, w3, sums, last):
    n_dev = back.shape[0]
    n_g, fan, tok = first.shape
    bw = w2.shape[2]
    n_q = w3.shape[0]
    gq = n_g // n_q
    last_local = ROWS // gq
    n_e = n_dev * last_local
    sum_shapes = [(n_g, fan, bw), (n_q, gq * bw, n_dev * ROWS)]
    out_shapes = [(n_g, fan + n_e, bw)] if last else sum_shapes
    n_out = len(out_shapes)

    def body(*refs):
        (turn_ref, first_ref, back_ref, w2_ref, w2t_ref, w3_ref), refs = refs[:6], refs[6:]
        start_refs, refs = refs[: len(sums)], refs[len(sums) :]
        slope_ref, *out_refs = refs[: n_out + 1]
        hid_ref, *acc_refs = refs[n_out + 1 :]
        acc_refs = acc_refs if last else out_refs
        acc2_ref, acc3_ref = acc_refs
        t = pl.program_id(0)

        @pl.when(t == 0)
        def _():
            for i in range(2):
                start = start_refs[i][...] if sums else jnp.zeros_like(acc_refs[i])
                acc_refs[i][...] = start

        @pl.loop(0, n_q, unroll=n_q)
        def _(q):
            held = back_ref[:, pl.ds(q * ROWS, ROWS), :].reshape(n_dev * ROWS, TILE)
            both, slopes = [], []
            for j in range(gq):
                g = q * gq + j
                pre = nn(w2t_ref[g], first_ref[g])
                cdf = 0.5 * (1.0 + lax.erf(pre * SQRT_HALF))
                hid_ref[j * bw : (j + 1) * bw, :] = (pre * cdf).astype(BF16)
                rise = cdf + pre * jnp.exp(-0.5 * pre * pre) * INV_SQRT_2PI
                back_hidden = nn(w3_ref[q, j * bw : (j + 1) * bw, :], held)
                slope = (back_hidden * rise).astype(BF16)
                slopes.append(slope)
                both.append(nn(w2_ref[g], slope).reshape(fan // SUB, SUB, TILE))
                if j % 2:
                    left = first_ref[pl.ds(g - 1, 2)].reshape(2 * fan, TILE)
                    prod = nt(left, jnp.concatenate(slopes, axis=0))
                    acc2_ref[g - 1] += prod[:fan, :bw]
                    acc2_ref[g] += prod[fan:, bw:]
                    at = pl.multiple_of((g - 1) * SUB, ROWS)
                    pair = jnp.concatenate(both, axis=1).astype(BF16)
                    slope_ref[:, pl.ds(at, ROWS), :] = pair
                    both, slopes = [], []
            acc3_ref[q] += nt(hid_ref[...], held)

        @pl.when(t == pl.num_programs(0) - 1 if last else False)
        def _():
            turn_g = turn_ref[1]
            col = lax.broadcasted_iota(jnp.int32, (n_e, n_dev * ROWS), 1)
            entry = lax.broadcasted_iota(jnp.int32, (n_e, n_dev * ROWS), 0)
            pick = (col // ROWS * last_local + col % last_local == entry).astype(F32)
            lane = lax.broadcasted_iota(jnp.int32, (bw, n_dev * ROWS), 1) % ROWS // last_local

            @pl.loop(0, n_q)
            def _(q):
                for j in range(gq):
                    g = q * gq + j
                    to = g ^ turn_g
                    out_refs[0][to, :fan, :] = acc2_ref[g]
                    rows = jnp.where(lane == j, acc3_ref[q, j * bw : (j + 1) * bw, :], 0.0)
                    out_refs[0][to, fan:, :] = lax.dot_general(
                        pick,
                        rows,
                        (((1,), (1,)), ((), ())),
                        precision=lax.Precision.HIGHEST,
                        preferred_element_type=F32,
                    )

    slope_shape = (fan // SUB, n_g * SUB, tok)
    return call(
        body,
        tok // TILE,
        [smem(), tokens_last(first.shape), tokens_last(back.shape)]
        + [whole(a.shape) for a in (w2, w2_t, w3, *sums)],
        [tokens_last(slope_shape)] + [whole(shape) for shape in out_shapes],
        [jax.ShapeDtypeStruct(slope_shape, BF16)]
        + [jax.ShapeDtypeStruct(shape, F32) for shape in out_shapes],
        [pltpu.VMEM((gq * bw, TILE), BF16)]
        + [pltpu.VMEM(shape, F32) for shape in sum_shapes if last],
        2 * tok * 6 * n_g * bw * fan,
        2 * (2 * first.size + back.size),
    )(turns, first, back, w2, w2_t, w3, *sums)


def first_grad(pieces, order, row, turns, slope, n_g, in_width, held_sum, last):
    n_piece, rows, tok = slope.shape
    depth1 = pieces[0].shape[1]
    n_a = depth1 // in_width
    spread = SUB // n_a
    sums = [] if held_sum is None else [held_sum]
    sum_shape = (n_piece, rows, in_width)
    out_shape = (2 * n_a, n_piece // 2, spread, n_g, in_width) if last else sum_shape

    def body(*refs):
        x_refs, refs = refs[:n_piece], refs[n_piece:]
        (order_ref, turn_ref, slope_ref), refs = refs[:3], refs[3:]
        start_refs, out_ref = refs[: len(sums)], refs[len(sums)]
        acc_ref = refs[-1]
        t = pl.program_id(0)

        @pl.when(t == 0)
        def _():
            acc_ref[...] = start_refs[0][...] if sums else jnp.zeros_like(acc_ref)

        owner = lax.broadcasted_iota(jnp.int32, (rows, in_width), 0) // spread % n_a
        for k in range(n_piece):
            p = order_ref[k]
            prod = nn(slope_ref[p], x_refs[k][...])
            total = acc_ref[p]
            for a in range(n_a):
                total += jnp.where(owner == a, prod[:, a * in_width : (a + 1) * in_width], 0.0)
            acc_ref[p] = total

        @pl.when(t == pl.num_programs(0) - 1 if last else False)
        def _():
            turn_a = turn_ref[0]
            for p in range(n_piece):
                for r in range(SUB):
                    a = p % 2 * n_a + r // spread
                    picked = acc_ref[p, pl.ds(r, n_g, stride=SUB), :]
                    out_ref[a ^ turn_a, p // 2, r % spread] = picked

    return call(
        body,
        tok // TILE,
        [piece_spec(p.shape, row) for p in pieces]
        + [smem(), smem(), tokens_last(slope.shape)]
        + [whole(a.shape) for a in sums],
        whole(out_shape),
        jax.ShapeDtypeStruct(out_shape, F32),
        [pltpu.VMEM(sum_shape, F32)] if last else [],
        2 * tok * n_piece * rows * depth1,
        2 * (n_piece * depth1 * tok + slope.size),
    )(*pieces, order, turns, slope, *sums)


def rows_to_out(rows_by_part):
    return jnp.concatenate([r.astype(F32) for r in rows_by_part], axis=0).T


def unpack_first(parts, spread):
    n_dev, local, _, n_g, in_width = parts.shape

    def body(in_ref, out_ref):
        out_ref[0] = rows_to_out([in_ref[d, 0, x] for x in range(spread) for d in range(n_dev)])

    out_cols = spread * n_dev * n_g
    return pl.pallas_call(
        body,
        grid=(local,),
        in_specs=[pl.BlockSpec((n_dev, 1, spread, n_g, in_width), lambda a: (0, a, 0, 0, 0))],
        out_specs=pl.BlockSpec((1, in_width, out_cols), lambda a: (a, 0, 0)),
        out_shape=jax.ShapeDtypeStruct((local, in_width, out_cols), F32),
        compiler_params=pltpu.CompilerParams(vmem_limit_bytes=VMEM_BYTES),
    )(parts)


def in_vmem():
    return pl.BlockSpec(memory_space=pltpu.VMEM)


def unpack_ring_first(halves, me, spread):
    n_dev, _, n_g, in_width = halves[0][0].shape
    local = 2 * len(halves[0])

    def body(me_ref, *refs):
        ins, out_ref = refs[:-1], refs[-1]
        for h in range(2):
            for k in range(local // 2):
                piece = ins[h * (local // 2) + k]
                rows = [piece[d, x] for x in range(spread) for d in range(n_dev)]
                out_ref[(me_ref[0] ^ k) * 2 + h] = rows_to_out(rows)

    return pl.pallas_call(
        body,
        in_specs=[smem()] + [in_vmem()] * local,
        out_specs=in_vmem(),
        out_shape=jax.ShapeDtypeStruct((local, in_width, spread * n_dev * n_g), F32),
        compiler_params=pltpu.CompilerParams(vmem_limit_bytes=VMEM_BYTES),
    )(me, *halves[0], *halves[1])


def unpack_ring_rest(halves, me, fan):
    some, rows, bw = halves[0][0].shape
    n_own = len(halves[0])
    n_g = 2 * n_own * some

    def body(me_ref, *refs):
        ins, (g2_ref, g3_ref) = refs[:-2], refs[-2:]
        for h in range(2):
            for k in range(n_own):
                piece = ins[h * n_own + k]
                base = ((me_ref[0] ^ k) * 2 + h) * some
                for j in range(some):
                    g2_ref[base + j] = piece[j, :fan, :].astype(F32)
                    g3_ref[base + j] = piece[j, fan:, :].astype(F32)

    return pl.pallas_call(
        body,
        in_specs=[smem()] + [in_vmem()] * (2 * n_own),
        out_specs=[in_vmem(), in_vmem()],
        out_shape=[
            jax.ShapeDtypeStruct((n_g, fan, bw), F32),
            jax.ShapeDtypeStruct((n_g, rows - fan, bw), F32),
        ],
        compiler_params=pltpu.CompilerParams(vmem_limit_bytes=VMEM_BYTES),
    )(me, *halves[0], *halves[1])


def swap(x):
    return lax.all_to_all(x, "blk", split_axis=0, concat_axis=0, tiled=True)


def turn(x, axis, bits):
    n = lax.axis_size(axis)
    return lax.ppermute(x, axis, [(i, i ^ bits) for i in range(n)])


def follow(x, *before):
    return lax.optimization_barrier((x, before))[0]


SIDES = ((1, 3), (3, 1))


def ring_send(parts, near):
    return turn(jnp.stack([parts[near], parts[2]]).astype(BF16), "tok", near)


def ring_half(parts, got, far):
    mine = parts[0] + got[0].astype(F32)
    theirs = parts[far] + got[1].astype(F32)
    return mine, turn(theirs.astype(BF16), "tok", far)


def ring_scatter(parts, near, far):
    mine, got = ring_half(parts, ring_send(parts, near), far)
    return mine + got.astype(F32)


def ring_gather(mine, near, far):
    other = turn(mine, "tok", far)
    got = turn(jnp.stack([mine, other]), "tok", near)
    parts = {0: mine, far: other, near: got[0], 2: got[1]}
    return [parts[k] for k in range(4)]


def gather_pieces(x, hold):
    half = x.shape[1] // 2
    low, high = x[:, :half], x[:, half:]
    one = [turn(p, "blk", 2) for p in (low, high)]
    two = [turn(p, "blk", 4) for p in (low, high)]
    one, two = follow((one, two), hold)
    both = [turn(one[0], "blk", 4), turn(two[1], "blk", 2)]
    pieces = []
    for group in ((low, high), one, two, both):
        pieces.extend(group)
        pieces.extend(turn(p, "blk", 1) for p in group)
    return pieces


def shards(cuts, student_in, teacher_out, w_first, w_second, w_third, w_fourth):
    n_dev = lax.axis_size("blk")
    n_tok = lax.axis_size("tok")
    tok_rows = student_in.shape[0]
    first_local, in_width, first_cols = w_first.shape
    n_first = first_local * n_dev
    n_g, fan, bw = w_second.shape
    n_second = n_g * n_dev
    spread = first_cols // n_second
    last_local, _, out_width = w_fourth.shape
    factor = 1.0 / float(tok_rows * n_tok) ** 0.5
    n_a = SUB // spread
    n_piece = n_first // n_a
    gq = ROWS // last_local
    n_q = n_g // gq
    me_tok = lax.axis_index("tok").astype(jnp.int32)
    ring = n_tok == 4 and first_local == 8 and n_g % 8 == 0
    turns = jnp.array([2, n_g // 4], jnp.int32) * (me_tok if ring else 0)

    n_chunks = len(cuts) - 1
    bounds = [(tok_rows * lo // cuts[-1], tok_rows * hi // cuts[-1]) for lo, hi in zip(cuts, cuts[1:])]

    cols = w_first.reshape(first_local, in_width, spread, n_dev, n_g).transpose(3, 0, 2, 4, 1)
    cols = swap(cols)
    w2_t = w_second.transpose(0, 2, 1)
    same_g = jnp.eye(gq, dtype=BF16)[None, :, None, None, :, None]
    w3_big = w_third.reshape(n_q, gq, bw, n_dev, 1, last_local) * same_g
    w3_big = w3_big.reshape(n_q, gq * bw, n_dev * ROWS)
    w3_t = w3_big.transpose(0, 2, 1)
    same_e = jnp.eye(last_local, dtype=BF16)[None, :, :, None]
    w4_big = (w_fourth.transpose(1, 0, 2)[:, :, None, :] * same_e).reshape(
        n_second * last_local, last_local * out_width
    )
    w4_t = w4_big.T
    w3_t, w4_big, w4_t = [follow(w, cols) for w in (w3_t, w4_big, w4_t)]
    w1 = cols.reshape(n_piece, n_a, spread, n_g, in_width).transpose(0, 3, 1, 2, 4)
    w1 = w1.reshape(n_piece, n_g * SUB, in_width)
    w1 = follow(w1, w3_t, w4_big, w4_t)

    order = jnp.arange(n_piece, dtype=jnp.int32)
    if n_dev == 8 and first_local == 2 * n_a:
        order = order ^ (2 * lax.axis_index("blk")).astype(jnp.int32)
        pieces = gather_pieces(student_in, (w1, w3_big, w3_t, w4_big, w4_t))
    else:
        x_all = lax.all_gather(student_in, "blk", axis=0)
        pieces = [p for d in range(n_dev) for p in jnp.split(x_all[d], n_piece // n_dev, axis=1)]

    firsts, thirds, backs, slopes, own_rest = [], [], [], [], []
    sums = ()
    grad_four = part_one = None
    done = ()

    def do_forward(c):
        nonlocal done
        first, third = forward(pieces, follow(order, done), bounds[c], w1, w2_t, w3_t, n_dev)
        firsts.append(first)
        thirds.append(swap(third))
        done = third

    def do_middle(c):
        nonlocal done, grad_four
        back, grad_four = middle(
            follow(thirds[c], done), teacher_out, bounds[c][0], w4_big, w4_t, factor, last_local,
            grad_four, c == n_chunks - 1,
        )
        backs.append(swap(back))
        done = back

    def do_backward(c):
        nonlocal done, sums
        slope, *sums = backward(
            follow(turns, done), firsts[c], backs[c], w_second, w2_t, w3_big, sums, c == n_chunks - 1
        )
        slopes.append(slope)
        done = slope

    def do_first_grad(c):
        nonlocal done, part_one, grad_four
        last = c == n_chunks - 1
        part_one = first_grad(
            pieces, order, bounds[c][0], follow(turns, done), slopes[c], n_g, in_width, part_one, last
        )
        done = part_one

    ring_state = {}

    def do_ring(c):
        nonlocal done
        if not ring:
            return
        if c == 0:
            rest = sums[0].reshape(4, 2, n_g // 8, *sums[0].shape[1:])
            ring_state["parts"] = [rest[:, h] for h in range(2)]
            ring_state["got"] = [ring_send(rest[:, h], SIDES[h][0]) for h in range(2)]
            return
        got = follow(ring_state["got"], done)
        if c == 1:
            halves = [ring_half(ring_state["parts"][h], got[h], SIDES[h][1]) for h in range(2)]
            ring_state["mine"], ring_state["got"] = zip(*halves)
            done = (done, ring_state["mine"])
            return
        pairs = zip(ring_state["mine"], got)
        own_rest.extend((mine + part.astype(F32)).astype(BF16) for mine, part in pairs)

    four = {}

    def do_ring_four(c):
        nonlocal done, grad_four
        if not ring:
            return
        near, far = SIDES[0]
        rank = me_tok ^ jnp.arange(4)
        if c == 0:
            four["shape"] = grad_four.shape
            parts = jnp.take(grad_four.reshape(4, -1, LANES), rank, axis=0)
            four["parts"], four["got"] = parts, ring_send(parts, near)
        elif c == 1:
            got = follow(four["got"], done)
            four["mine"], four["got"] = ring_half(four["parts"], got, far)
            done = (done, four["mine"])
        elif c == 2:
            got = follow(four["got"], done)
            four["own"] = (four["mine"] + got.astype(F32)).astype(BF16)
            four["other"] = turn(four["own"], "tok", far)
            done = (done, four["own"])
        elif c == 3:
            pair = jnp.stack([four["own"], follow(four["other"], done)])
            four["pair"], four["got"] = pair, turn(pair, "tok", near)
            done = (done, pair)
        else:
            pair, got = four["pair"], follow(four["got"], done)
            parts = {0: pair[0], far: pair[1], near: got[0], 2: got[1]}
            parts = jnp.stack([parts[k] for k in range(4)])
            grad_four = jnp.take(parts, rank, axis=0).reshape(four["shape"]).astype(F32)

    steps = {
        "q": do_ring_four,
        "r": do_ring,
        "f": do_forward,
        "m": do_middle,
        "b": do_backward,
        "x": do_first_grad,
    }
    for step in PLAN:
        steps[step[0]](int(step[1]))
    rest = sums[0]
    if not ring:
        grad_four, rest = lax.psum((grad_four.astype(BF16), rest.astype(BF16)), "tok")
        grad_two, grad_three = rest[:, :fan].astype(F32), rest[:, fan:].astype(F32)
        part_one = part_one.transpose(1, 0, 2, 3, 4)
        part_one = part_one.reshape(n_dev, first_local, spread, n_g, in_width).astype(BF16)
        grad_one = unpack_first(lax.psum(swap(part_one), "tok"), spread)
        return (grad_one, grad_two, grad_three.transpose(0, 2, 1), grad_four.astype(F32))

    me = me_tok.reshape(1)
    rest_halves = [ring_gather(own_rest[h], *SIDES[h]) for h in range(2)]
    grad_two, grad_three = unpack_ring_rest(rest_halves, me, fan)
    one = part_one.reshape(4, 2, n_dev, spread, n_g, in_width)
    own = [ring_scatter(one[:, h], *SIDES[h]).astype(BF16) for h in range(2)]
    own = swap(jnp.stack(own, axis=1))
    one_halves = [ring_gather(own[:, h], *SIDES[h]) for h in range(2)]
    grad_one = unpack_ring_first(one_halves, me, spread)
    return (grad_one, grad_two, grad_three.transpose(0, 2, 1), grad_four)


def solution(mesh):
    placed = (
        P("tok", "blk"),
        P("tok", "blk"),
        P("blk", None, None),
        P("blk", None, None),
        P("blk", None, None),
        P("blk", None, None),
    )
    return jax.shard_map(
        functools.partial(shards, CUTS),
        mesh=mesh,
        in_specs=placed,
        out_specs=(
            P("blk", None, None),
            P("blk", None, None),
            P("blk", None, None),
            P("blk", None, None),
        ),
        check_vma=False,
    )
```

time: 902 us -> 459 us (0.51)
  blocking collectives: 214 us -> 0 us
  waiting for transfers between devices: 366 us -> 174 us
  matrix products: 159 us -> 0 us
  Pallas kernels: 0 us -> 157 us
  local copies, waits for them, and re-layouts: 132 us -> 28.9 us
  starting transfers between devices: 10.8 us -> 76.1 us
  other arithmetic: 0.01 us -> 17.5 us
  between operations: 14.6 us -> 1.6 us
    all_to_all x2 -> x0, blocking collectives: 214 us -> none  [the longest x1 167 us: shards(): lax.all_to_all(first_view, 'blk', split_axis=2, concat_axis=0, tiled=True)]
    psum x1 -> x0, waiting for transfers between devices: 207 us -> none  [shards(): lax.psum((grad_part, grad_two, grad_three, grad_four), 'tok')]
    dot_general x11 -> x0, matrix products: 159 us -> none  [the longest x1 70.5 us: shards(): jnp.einsum('axgt,gaxo->got', mixed, second_view, preferred_element_type=f32)]
    pallas_call x0 -> x10, Pallas kernels: none -> 157 us  [the longest x2 67.7 us: backward(): call(body, tok // TILE, [smem(), tokens_last(first.shape), tokens_last(ba...]
    ppermute x0 -> x34, waiting for transfers between devices: none -> 79.3 us  [turn(): return lax.ppermute(x, axis, [(i, i ^ bits) for i in range(n)])]
    all_to_all x2 -> x6, waiting for transfers between devices: 160 us -> 94.8 us  [swap(): return lax.all_to_all(x, 'blk', split_axis=0, concat_axis=0, tiled=True)]
    ppermute x0 -> x34, starting transfers between devices: none -> 42 us  [turn(): return lax.ppermute(x, axis, [(i, i ^ bits) for i in range(n)])]
    convert_element_type x4 -> x1, local copies, waits for them, and re-layouts: 38.8 us -> 0.11 us  [shards(): same_g = jnp.eye(gq, dtype=BF16)[None, :, None, None, :, None]]
  transfers between devices with their start and end apart: 3 -> 40, of which waited for: 3 -> 18; matrix products, arithmetic and copies ran while one was open for 5% -> 9% of each run, Pallas kernels for 0% -> 31%
where the time goes in v1:
time: 459 us; the launch traced here: 455 us
  waiting for transfers between devices  174 us (38%)
  Pallas kernels  157 us (34%)
  starting transfers between devices  76.1 us (17%)
  local copies, waits for them, and re-layouts  28.9 us (6%)
  other arithmetic  17.5 us (4%)
    all_to_all x6, waiting for transfers between devices, swap(): return lax.all_to_all(x, 'blk', split_axis=0, concat_axis=0, tiled=True)  94.8 us
    ppermute x34, waiting for transfers between devices, turn(): return lax.ppermute(x, axis, [(i, i ^ bits) for i in range(n)])  79.3 us
    pallas_call x2, Pallas kernels, backward(): call(body, tok // TILE, [smem(), tokens_last(first.shape), tokens_last(ba...  67.7 us
    ppermute x34, starting transfers between devices, turn(): return lax.ppermute(x, axis, [(i, i ^ bits) for i in range(n)])  42 us
    all_to_all x6, starting transfers between devices, swap(): return lax.all_to_all(x, 'blk', split_axis=0, concat_axis=0, tiled=True)  34.2 us
    pallas_call x2, Pallas kernels, forward(): call(body, tok // TILE, [piece_spec(p.shape, span[0]) for p in pieces] +...  32.6 us
    pallas_call x2, Pallas kernels, middle(): call(body, tok // TILE, [tokens_last(third.shape), pl.BlockSpec((TILE, co...  27.8 us
    pallas_call x2, Pallas kernels, first_grad(): call(body, tok // TILE, [piece_spec(p.shape, row) for p in pieces] + [sme...  23 us
  transfers between devices with their start and end apart: 40, of which 18 were waited for; matrix products, arithmetic and copies ran while one was open for 9% of the time, Pallas kernels for 31%

profile of v1, /device:TPU:0, one launch (start us, length us, event | category | flops | bytes accessed | tf_op | source)
XLA Modules:
  0.0 455.4 jit_solution(16356909149439548266)
XLA Ops:
  11.9 4.5 all-to-all-start
  23.4 4.0 copy.39
  29.5 69.5 %all-to-all-done = bf16[8,8,2,32,128]{4,3,2,1,0:T(8,128)(2,1)} async-done(((bf16[8,8,2,32,128]{4,3,2,1,0:T(8,128)(2,1)}), bf16[8,8,2,32,128]{4,3,2,1,0:T(8,128)(2,1)}, u32[]{:S(2)}, u32[]{:S(2)}) %all-to-all-start) | async-done | bytes 1048608 | tf_op jit(solution)/shard_map/all_to_all | solution.py:394
  109.2 36.0 %collective-permute-done.10.refs_12_ = bf16[1792,512]{1,0:T(8,128)(2,1)} collective-permute-done((bf16[1792,512]{1,0:T(8,128)(2,1)}, bf16[1792,512]{1,0:T(8,128)(2,1)}, u32[]{:S(2)}, u32[]{:S(2)}) %collective-permute-start.10) | collective-permute-done | bytes 1835040 | tf_op jit(solution)/shard_map/ppermute | solution.py:399
  152.1 14.7 %shard_map.102 = (bf16[32,128,768]{2,1,0:T(8,128)(2,1)}, bf16[8,128,768]{2,1,0:T(8,128)(2,1)}) custom-call(bf16[1792,512]{1,0:T(8,128)(2,1)} %get-tuple-element.81.refs_0_, bf16[1792,512]{1,0:T(8,128)(2,1)} %copy-done, bf16[1792,512]{1,0:T(8,128)(2,1)} %collective-permute-done.refs_2_, bf16[1792,512]{1,0:T(8,128)(2,1)} %collective-permute-done.1.refs_3_, ...), custom_call_target="tpu_custom_call" | custom-call | flops 4831838208 | bytes 19922944 | tf_op jit(solution)/shard_map/pallas_call | solution.py:105
  166.8 13.5 %all-to-all-start.2 = ((bf16[8,128,768]{2,1,0:T(8,128)(2,1)}), bf16[8,128,768]{2,1,0:T(8,128)(2,1)S(1)}, u32[]{:S(2)}, u32[]{:S(2)}) async-start(bf16[8,128,768]{2,1,0:T(8,128)(2,1)} %get-tuple-element.50), calls=%async_computation.2 | async-start | bytes 3145728 | tf_op jit(solution)/shard_map/all_to_all | solution.py:394
  180.2 17.9 %shard_map.103 = (bf16[32,128,1024]{2,1,0:T(8,128)(2,1)}, bf16[8,128,1024]{2,1,0:T(8,128)(2,1)}) custom-call(bf16[1792,512]{1,0:T(8,128)(2,1)} %get-tuple-element.81.refs_0_, bf16[1792,512]{1,0:T(8,128)(2,1)} %copy-done, bf16[1792,512]{1,0:T(8,128)(2,1)} %collective-permute-done.refs_2_, bf16[1792,512]{1,0:T(8,128)(2,1)} %collective-permute-done.1.refs_3_, ...), custom_call_target="tpu_custom_call" | custom-call | flops 6442450944 | bytes 26214400 | tf_op jit(solution)/shard_map/pallas_call | solution.py:105
  202.1 3.6 all-to-all-start.1
  205.7 12.3 %shard_map.104 = (bf16[8,128,768]{2,1,0:T(8,128)(2,1)}, f32[2,1024,128]{2,1,0:T(8,128)}) custom-call(bf16[8,128,768]{2,1,0:T(8,128)(2,1)} %copy-done.6, bf16[1792,1024]{1,0:T(8,128)(2,1)} %teach_ref.3, bf16[1024,1024]{1,0:T(8,128)(2,1)} %bitcast.190, bf16[1024,1024]{1,0:T(8,128)(2,1)} %bitcast.196), custom_call_target="tpu_custom_call" | custom-call | flops 4831838208 | bytes 8912896 | tf_op jit(solution)/shard_map/pallas_call | solution.py:159
  218.1 14.2 %all-to-all-done.1.third_ref = bf16[8,128,1024]{2,1,0:T(8,128)(2,1)S(1)} async-done(((bf16[8,128,1024]{2,1,0:T(8,128)(2,1)}), bf16[8,128,1024]{2,1,0:T(8,128)(2,1)S(1)}, u32[]{:S(2)}, u32[]{:S(2)}) %all-to-all-start.1) | async-done | bytes 2097184 | tf_op jit(solution)/shard_map/all_to_all | solution.py:394
  232.3 4.3 all-to-all-start.3
  236.6 15.5 %shard_map.105 = (bf16[8,128,1024]{2,1,0:T(8,128)(2,1)}, f32[4,256,256]{2,1,0:T(8,128)}) custom-call(bf16[8,128,1024]{2,1,0:T(8,128)(2,1)} %copy-done.5, bf16[1792,1024]{1,0:T(8,128)(2,1)} %teach_ref.3, bf16[1024,1024]{1,0:T(8,128)(2,1)} %bitcast.191, bf16[1024,1024]{1,0:T(8,128)(2,1)} %bitcast.197, f32[2,1024,128]{2,1,0:T(8,128)} %get-tuple-element.56.refs_0_), custom_call_target="tpu_custom_call" | custom-call | flops 6442450944 | bytes 10485760 | tf_op jit(solution)/shard_map/pallas_call | solution.py:159
  252.1 5.6 %all-to-all-done.3.refs_2_ = bf16[8,128,768]{2,1,0:T(8,128)(2,1)} async-done(((bf16[8,128,768]{2,1,0:T(8,128)(2,1)}), bf16[8,128,768]{2,1,0:T(8,128)(2,1)}, u32[]{:S(2)}, u32[]{:S(2)}) %all-to-all-start.3) | async-done | bytes 1572896 | tf_op jit(solution)/shard_map/all_to_all | solution.py:394
  257.6 4.5 all-to-all-start.4
  265.4 27.5 %shard_map.106 = (bf16[16,256,768]{2,1,0:T(8,128)(2,1)}, f32[32,128,128]{2,1,0:T(8,128)}, f32[8,512,128]{2,1,0:T(8,128)}) custom-call(s32[2]{0:T(128)} %broadcast_multiply_fusion.2.refs_0_.refs_17_, bf16[32,128,768]{2,1,0:T(8,128)(2,1)} %get-tuple-element.59.refs_1_, bf16[8,128,768]{2,1,0:T(8,128)(2,1)} %all-to-all-done.3.refs_2_, ...), custom_call_target="tpu_custom_call" | custom-call | flops 4831838208 | bytes 14155776 | tf_op jit(solution)/shard_map/pallas_call | solution.py:253
  295.4 40.2 %shard_map.107 = (bf16[16,256,1024]{2,1,0:T(8,128)(2,1)}, f32[32,160,128]{2,1,0:T(8,128)}) custom-call(s32[2]{0:T(128)} %broadcast_multiply_fusion.2.refs_0_.refs_17_, bf16[32,128,1024]{2,1,0:T(8,128)(2,1)} %get-tuple-element.64.refs_1_, bf16[8,128,1024]{2,1,0:T(8,128)(2,1)} %all-to-all-done.4.refs_2_, bf16[32,128,128]{2,1,0:T(8,128)(2,1)} %refs_3_.3, ...), custom_call_target="tpu_custom_call" | custom-call | flops 6442450944 | bytes 18874368 | tf_op jit(solution)/shard_map/pallas_call | solution.py:253
  341.8 9.9 %shard_map.108.refs_19_ = f32[16,256,128]{2,1,0:T(8,128)} custom-call(bf16[1792,512]{1,0:T(8,128)(2,1)} %get-tuple-element.81.refs_0_, bf16[1792,512]{1,0:T(8,128)(2,1)} %copy-done, bf16[1792,512]{1,0:T(8,128)(2,1)} %collective-permute-done.refs_2_, bf16[1792,512]{1,0:T(8,128)(2,1)} %collective-permute-done.1.refs_3_, ...), custom_call_target="tpu_custom_call" | custom-call | flops 3221225472 | bytes 18874368 | tf_op jit(solution)/shard_map/pallas_call | solution.py:306
  352.9 4.8 %collective-permute-done.18 = bf16[2,4,160,128]{3,2,1,0:T(8,128)(2,1)S(1)} collective-permute-done((bf16[2,4,160,128]{3,2,1,0:T(8,128)(2,1)S(1)}, bf16[2,4,160,128]{3,2,1,0:T(8,128)(2,1)S(1)}, u32[]{:S(2)}, u32[]{:S(2)}) %collective-permute-start.18) | collective-permute-done | bytes 327712 | tf_op jit(solution)/shard_map/ppermute | solution.py:399
  360.6 13.1 %shard_map.109 = f32[8,8,2,32,128]{4,3,2,1,0:T(8,128)} custom-call(bf16[1792,512]{1,0:T(8,128)(2,1)} %get-tuple-element.81.refs_0_, bf16[1792,512]{1,0:T(8,128)(2,1)} %copy-done, bf16[1792,512]{1,0:T(8,128)(2,1)} %collective-permute-done.refs_2_, bf16[1792,512]{1,0:T(8,128)(2,1)} %collective-permute-done.1.refs_3_, ...), custom_call_target="tpu_custom_call" | custom-call | flops 4294967296 | bytes 25165824 | tf_op jit(solution)/shard_map/pallas_call | solution.py:306
  381.6 8.2 %collective-permute-done.19 = bf16[2,8,2,32,128]{4,3,2,1,0:T(8,128)(2,1)} collective-permute-done((bf16[2,8,2,32,128]{4,3,2,1,0:T(8,128)(2,1)}, bf16[2,8,2,32,128]{4,3,2,1,0:T(8,128)(2,1)}, u32[]{:S(2)}, u32[]{:S(2)}) %collective-permute-start.19) | collective-permute-done | bytes 262176 | tf_op jit(solution)/shard_map/ppermute | solution.py:399
  399.1 5.8 %collective-permute-start.22 = (bf16[8,2,32,128]{3,2,1,0:T(8,128)(2,1)S(1)}, bf16[8,2,32,128]{3,2,1,0:T(8,128)(2,1)S(1)}, u32[]{:S(2)}, u32[]{:S(2)}) collective-permute-start(bf16[8,2,32,128]{3,2,1,0:T(8,128)(2,1)S(1)} %get-tuple-element.89), channel_id=1, source_target_pairs={{0,8},{8,0},{16,24},{24,16},{1,9},{9,1},{17,25},{25,17},{2,10},{10... | collective-permute-start | bytes 393224 | tf_op jit(solution)/shard_map/ppermute | solution.py:399
  409.5 3.8 all-to-all-start.5
  424.6 12.2 %collective-permute-done.25.refs_5_ = bf16[8,2,32,128]{3,2,1,0:T(8,128)(2,1)S(1)} collective-permute-done((bf16[8,2,32,128]{3,2,1,0:T(8,128)(2,1)S(1)}, bf16[8,2,32,128]{3,2,1,0:T(8,128)(2,1)S(1)}, u32[]{:S(2)}, u32[]{:S(2)}) %collective-permute-start.25) | collective-permute-done | bytes 131104 | tf_op jit(solution)/shard_map/ppermute | solution.py:399
  443.4 4.6 %collective-permute-done.26 = bf16[2,8,2,32,128]{4,3,2,1,0:T(8,128)(2,1)S(1)} collective-permute-done((bf16[2,8,2,32,128]{4,3,2,1,0:T(8,128)(2,1)S(1)}, bf16[2,8,2,32,128]{4,3,2,1,0:T(8,128)(2,1)S(1)}, u32[]{:S(2)}, u32[]{:S(2)}) %collective-permute-start.26) | collective-permute-done | bytes 262176 | tf_op jit(solution)/shard_map/ppermute | solution.py:399
  (167 shorter events, 103.7 us)
Async XLA Ops:
  4.2 98.1 %collective-permute-start.5 = (bf16[1792,512]{1,0:T(8,128)(2,1)S(1)}, bf16[1792,512]{1,0:T(8,128)(2,1)}, u32[]{:S(2)}, u32[]{:S(2)}) collective-permute-start(bf16[1792,512]{1,0:T(8,128)(2,1)S(1)} %get-tuple-element.80.refs_1_), channel_id=1, source_target_pairs={{0,4},{1,5},{2,6},{3,7},{4,0},{5,1},{6,2},{7,3},{8,12},{9,13},{10,... | collective-permute-start | bytes 5505032 | tf_op jit(solution)/shard_map/ppermute | solution.py:399
  7.1 95.2 %collective-permute-start.3 = (bf16[1792,512]{1,0:T(8,128)(2,1)S(1)}, bf16[1792,512]{1,0:T(8,128)(2,1)}, u32[]{:S(2)}, u32[]{:S(2)}) collective-permute-start(bf16[1792,512]{1,0:T(8,128)(2,1)S(1)} %get-tuple-element.80.refs_1_), channel_id=1, source_target_pairs={{0,2},{1,3},{2,0},{3,1},{4,6},{5,7},{6,4},{7,5},{8,10},{9,11},{10,... | collective-permute-start | bytes 5505032 | tf_op jit(solution)/shard_map/ppermute | solution.py:399
  8.6 93.7 %collective-permute-start.4 = (bf16[1792,512]{1,0:T(8,128)(2,1)}, bf16[1792,512]{1,0:T(8,128)(2,1)}, u32[]{:S(2)}, u32[]{:S(2)}) collective-permute-start(bf16[1792,512]{1,0:T(8,128)(2,1)} %get-tuple-element.81.refs_0_), channel_id=1, source_target_pairs={{0,4},{1,5},{2,6},{3,7},{4,0},{5,1},{6,2},{7,3},{8,12},{9,13},{10,... | collective-permute-start | bytes 5505032 | tf_op jit(solution)/shard_map/ppermute | solution.py:399
  9.1 93.2 %collective-permute-start.2 = (bf16[1792,512]{1,0:T(8,128)(2,1)}, bf16[1792,512]{1,0:T(8,128)(2,1)}, u32[]{:S(2)}, u32[]{:S(2)}) collective-permute-start(bf16[1792,512]{1,0:T(8,128)(2,1)} %get-tuple-element.81.refs_0_), channel_id=1, source_target_pairs={{0,2},{1,3},{2,0},{3,1},{4,6},{5,7},{6,4},{7,5},{8,10},{9,11},{10,... | collective-permute-start | bytes 5505032 | tf_op jit(solution)/shard_map/ppermute | solution.py:399
  9.1 96.0 %collective-permute-start.1 = (bf16[1792,512]{1,0:T(8,128)(2,1)S(1)}, bf16[1792,512]{1,0:T(8,128)(2,1)}, u32[]{:S(2)}, u32[]{:S(2)}) collective-permute-start(bf16[1792,512]{1,0:T(8,128)(2,1)S(1)} %get-tuple-element.80.refs_1_), channel_id=1, source_target_pairs={{0,1},{1,0},{2,3},{3,2},{4,5},{5,4},{6,7},{7,6},{8,9},{9,8},{10,11... | collective-permute-start | bytes 5505032 | tf_op jit(solution)/shard_map/ppermute | solution.py:399
  11.9 87.1 %all-to-all-start = ((bf16[8,8,2,32,128]{4,3,2,1,0:T(8,128)(2,1)}), bf16[8,8,2,32,128]{4,3,2,1,0:T(8,128)(2,1)}, u32[]{:S(2)}, u32[]{:S(2)}) async-start(bf16[8,8,2,32,128]{4,3,2,1,0:T(8,128)(2,1)} %copy.32), calls=%async_computation | async-start | bytes 2097152 | tf_op jit(solution)/shard_map/all_to_all | solution.py:394
  102.9 42.3 %collective-permute-start.10 = (bf16[1792,512]{1,0:T(8,128)(2,1)}, bf16[1792,512]{1,0:T(8,128)(2,1)}, u32[]{:S(2)}, u32[]{:S(2)}) collective-permute-start(bf16[1792,512]{1,0:T(8,128)(2,1)} %collective-permute-done.2.refs_4_), channel_id=1, source_target_pairs={{0,4},{1,5},{2,6},{3,7},{4,0},{5,1},{6,2},{7,3},{8,12},{9,13},{10,... | collective-permute-start | bytes 5505032 | tf_op jit(solution)/shard_map/ppermute | solution.py:399
  104.6 42.0 %collective-permute-start.11 = (bf16[1792,512]{1,0:T(8,128)(2,1)}, bf16[1792,512]{1,0:T(8,128)(2,1)}, u32[]{:S(2)}, u32[]{:S(2)}) collective-permute-start(bf16[1792,512]{1,0:T(8,128)(2,1)} %collective-permute-done.5.refs_9_), channel_id=1, source_target_pairs={{0,2},{1,3},{2,0},{3,1},{4,6},{5,7},{6,4},{7,5},{8,10},{9,11},{10,... | collective-permute-start | bytes 5505032 | tf_op jit(solution)/shard_map/ppermute | solution.py:399
  105.2 45.6 %collective-permute-start.6 = (bf16[1792,512]{1,0:T(8,128)(2,1)}, bf16[1792,512]{1,0:T(8,128)(2,1)S(1)}, u32[]{:S(2)}, u32[]{:S(2)}) collective-permute-start(bf16[1792,512]{1,0:T(8,128)(2,1)} %collective-permute-done.2.refs_4_), channel_id=1, source_target_pairs={{0,1},{1,0},{2,3},{3,2},{4,5},{5,4},{6,7},{7,6},{8,9},{9,8},{10,11... | collective-permute-start | bytes 5505032 | tf_op jit(solution)/shard_map/ppermute | solution.py:399
  106.4 44.3 %collective-permute-start.9 = (bf16[1792,512]{1,0:T(8,128)(2,1)}, bf16[1792,512]{1,0:T(8,128)(2,1)}, u32[]{:S(2)}, u32[]{:S(2)}) collective-permute-start(bf16[1792,512]{1,0:T(8,128)(2,1)} %collective-permute-done.5.refs_9_), channel_id=1, source_target_pairs={{0,1},{1,0},{2,3},{3,2},{4,5},{5,4},{6,7},{7,6},{8,9},{9,8},{10,11... | collective-permute-start | bytes 5505032 | tf_op jit(solution)/shard_map/ppermute | solution.py:399
  109.0 41.7 %collective-permute-start.8 = (bf16[1792,512]{1,0:T(8,128)(2,1)}, bf16[1792,512]{1,0:T(8,128)(2,1)}, u32[]{:S(2)}, u32[]{:S(2)}) collective-permute-start(bf16[1792,512]{1,0:T(8,128)(2,1)} %collective-permute-done.4.refs_8_), channel_id=1, source_target_pairs={{0,1},{1,0},{2,3},{3,2},{4,5},{5,4},{6,7},{7,6},{8,9},{9,8},{10,11... | collective-permute-start | bytes 5505032 | tf_op jit(solution)/shard_map/ppermute | solution.py:399
  166.8 34.2 %all-to-all-start.2 = ((bf16[8,128,768]{2,1,0:T(8,128)(2,1)}), bf16[8,128,768]{2,1,0:T(8,128)(2,1)S(1)}, u32[]{:S(2)}, u32[]{:S(2)}) async-start(bf16[8,128,768]{2,1,0:T(8,128)(2,1)} %get-tuple-element.50), calls=%async_computation.2 | async-start | bytes 3145728 | tf_op jit(solution)/shard_map/all_to_all | solution.py:394
  202.1 30.2 %all-to-all-start.1 = ((bf16[8,128,1024]{2,1,0:T(8,128)(2,1)}), bf16[8,128,1024]{2,1,0:T(8,128)(2,1)S(1)}, u32[]{:S(2)}, u32[]{:S(2)}) async-start(bf16[8,128,1024]{2,1,0:T(8,128)(2,1)} %get-tuple-element.52), calls=%async_computation.1 | async-start | bytes 4194304 | tf_op jit(solution)/shard_map/all_to_all | solution.py:394
  232.3 25.3 %all-to-all-start.3 = ((bf16[8,128,768]{2,1,0:T(8,128)(2,1)}), bf16[8,128,768]{2,1,0:T(8,128)(2,1)}, u32[]{:S(2)}, u32[]{:S(2)}) async-start(bf16[8,128,768]{2,1,0:T(8,128)(2,1)} %get-tuple-element.54), calls=%async_computation.3 | async-start | bytes 3145728 | tf_op jit(solution)/shard_map/all_to_all | solution.py:394
  257.6 37.8 %all-to-all-start.4 = ((bf16[8,128,1024]{2,1,0:T(8,128)(2,1)}), bf16[8,128,1024]{2,1,0:T(8,128)(2,1)}, u32[]{:S(2)}, u32[]{:S(2)}) async-start(bf16[8,128,1024]{2,1,0:T(8,128)(2,1)} %get-tuple-element.57), calls=%async_computation.4 | async-start | bytes 4194304 | tf_op jit(solution)/shard_map/all_to_all | solution.py:394
  263.6 29.2 %collective-permute-start.14 = (bf16[2,512,128]{2,1,0:T(8,128)(2,1)S(1)}, bf16[2,512,128]{2,1,0:T(8,128)(2,1)S(1)}, u32[]{:S(2)}, u32[]{:S(2)}) collective-permute-start(bf16[2,512,128]{2,1,0:T(8,128)(2,1)S(1)} %stack.95), channel_id=1, source_target_pairs={{0,8},{8,0},{16,24},{24,16},{1,9},{9,1},{17,25},{25,17},{2,10},{10... | collective-permute-start | bytes 786440 | tf_op jit(solution)/shard_map/ppermute | solution.py:399
  292.9 42.8 %collective-permute-start.15 = (bf16[512,128]{1,0:T(8,128)(2,1)S(1)}, bf16[512,128]{1,0:T(8,128)(2,1)S(1)}, u32[]{:S(2)}, u32[]{:S(2)}) collective-permute-start(bf16[512,128]{1,0:T(8,128)(2,1)S(1)} %get-tuple-element.94), channel_id=1, source_target_pairs={{0,24},{8,16},{16,8},{24,0},{1,25},{9,17},{17,9},{25,1},{2,26},{10... | collective-permute-start | bytes 393224 | tf_op jit(solution)/shard_map/ppermute | solution.py:399
  339.2 18.4 %collective-permute-start.18 = (bf16[2,4,160,128]{3,2,1,0:T(8,128)(2,1)S(1)}, bf16[2,4,160,128]{3,2,1,0:T(8,128)(2,1)S(1)}, u32[]{:S(2)}, u32[]{:S(2)}) collective-permute-start(bf16[2,4,160,128]{3,2,1,0:T(8,128)(2,1)S(1)} %pad_maximum_fusion.2), channel_id=1, source_target_pairs={{0,24},{8,16},{16,8},{24,0},{1,25},{9,17},{17,9},{25,1},{2,26},{10... | collective-permute-start | bytes 983048 | tf_op jit(solution)/shard_map/ppermute | solution.py:399
  351.7 27.9 %collective-permute-start.33 = (bf16[2,512,128]{2,1,0:T(8,128)(2,1)S(1)}, bf16[2,512,128]{2,1,0:T(8,128)(2,1)S(1)}, u32[]{:S(2)}, u32[]{:S(2)}) collective-permute-start(bf16[2,512,128]{2,1,0:T(8,128)(2,1)S(1)} %pad_maximum_fusion.5), channel_id=1, source_target_pairs={{0,8},{8,0},{16,24},{24,16},{1,9},{9,1},{17,25},{25,17},{2,10},{10... | collective-permute-start | bytes 786440 | tf_op jit(solution)/shard_map/ppermute | solution.py:399
  358.5 23.1 %collective-permute-start.28 = (bf16[4,160,128]{2,1,0:T(8,128)(2,1)}, bf16[4,160,128]{2,1,0:T(8,128)(2,1)}, u32[]{:S(2)}, u32[]{:S(2)}) collective-permute-start(bf16[4,160,128]{2,1,0:T(8,128)(2,1)} %get-tuple-element.82), channel_id=1, source_target_pairs={{0,8},{8,0},{16,24},{24,16},{1,9},{9,1},{17,25},{25,17},{2,10},{10... | collective-permute-start | bytes 491528 | tf_op jit(solution)/shard_map/ppermute | solution.py:399
  359.3 22.3 %collective-permute-start.27 = (bf16[4,160,128]{2,1,0:T(8,128)(2,1)}, bf16[4,160,128]{2,1,0:T(8,128)(2,1)}, u32[]{:S(2)}, u32[]{:S(2)}) collective-permute-start(bf16[4,160,128]{2,1,0:T(8,128)(2,1)} %get-tuple-element.87), channel_id=1, source_target_pairs={{0,24},{8,16},{16,8},{24,0},{1,25},{9,17},{17,9},{25,1},{2,26},{10... | collective-permute-start | bytes 491528 | tf_op jit(solution)/shard_map/ppermute | solution.py:399
  376.3 19.5 %collective-permute-start.21 = (bf16[2,8,2,32,128]{4,3,2,1,0:T(8,128)(2,1)}, bf16[2,8,2,32,128]{4,3,2,1,0:T(8,128)(2,1)}, u32[]{:S(2)}, u32[]{:S(2)}) collective-permute-start(bf16[2,8,2,32,128]{4,3,2,1,0:T(8,128)(2,1)} %pad_maximum_fusion.7), channel_id=1, source_target_pairs={{0,24},{8,16},{16,8},{24,0},{1,25},{9,17},{17,9},{25,1},{2,26},{10... | collective-permute-start | bytes 786440 | tf_op jit(solution)/shard_map/ppermute | solution.py:399
  394.2 19.1 %collective-permute-start.29 = (bf16[4,160,128]{2,1,0:T(8,128)(2,1)S(1)}, bf16[4,160,128]{2,1,0:T(8,128)(2,1)S(1)}, u32[]{:S(2)}, u32[]{:S(2)}) collective-permute-start(bf16[4,160,128]{2,1,0:T(8,128)(2,1)S(1)} %add_convert_fusion.1.refs_0_), channel_id=1, source_target_pairs={{0,24},{8,16},{16,8},{24,0},{1,25},{9,17},{17,9},{25,1},{2,26},{10... | collective-permute-start | bytes 491528 | tf_op jit(solution)/shard_map/ppermute | solution.py:399
  415.5 24.1 %collective-permute-start.32 = (bf16[2,4,160,128]{3,2,1,0:T(8,128)(2,1)S(1)}, bf16[2,4,160,128]{3,2,1,0:T(8,128)(2,1)S(1)}, u32[]{:S(2)}, u32[]{:S(2)}) collective-permute-start(bf16[2,4,160,128]{3,2,1,0:T(8,128)(2,1)S(1)} %pad_maximum_fusion.4), channel_id=1, source_target_pairs={{0,24},{8,16},{16,8},{24,0},{1,25},{9,17},{17,9},{25,1},{2,26},{10... | collective-permute-start | bytes 983048 | tf_op jit(solution)/shard_map/ppermute | solution.py:399
  (36 other events, 466.7 us)

commit v2 on v1

--- a/solution.py
+++ b/solution.py
@@ -11,7 +11,7 @@
 BF16 = jnp.bfloat16
 TILE = 256
 CUTS = (0, 3, 7)
-PLAN = ("f0", "f1", "m0", "m1", "q0", "b0", "q1", "b1", "q2", "r0", "x0", "q3", "r1", "x1", "r2", "q4")
+PLAN = ("g0", "h0", "f0", "g1", "m0", "h1", "f1", "s0", "m1", "q0", "d0", "q1", "x0", "s1", "q2", "x1", "q3", "r0", "d1", "q4", "r1")
 ROWS = 16
 SUB = 8
 LANES = 128
@@ -37,8 +37,8 @@
     return pl.BlockSpec(shape[:-1] + (TILE,), lambda t: (0,) * lead + (t,))
 
 
-def piece_spec(shape, row):
-    return pl.BlockSpec((TILE, shape[1]), lambda t: (t + row // TILE, 0))
+def piece_spec(shape):
+    return pl.BlockSpec((TILE, shape[1]), lambda t: (t, 0))
 
 
 def smem():
@@ -58,9 +58,9 @@
     )
 
 
-def forward(pieces, order, span, w1, w2_t, w3_t, n_dev):
+def forward(pieces, order, w1, w2_t, w3_t, n_dev):
     n_piece, rows1, in_width = w1.shape
-    tok = span[1] - span[0]
+    tok = pieces[0].shape[0]
     depth1 = pieces[0].shape[1]
     n_a = depth1 // in_width
     n_g, bw, fan = w2_t.shape
@@ -105,7 +105,7 @@
     return call(
         body,
         tok // TILE,
-        [piece_spec(p.shape, span[0]) for p in pieces]
+        [piece_spec(p.shape) for p in pieces]
         + [smem(), whole(w1.shape), whole(w2_t.shape), whole(w3_t.shape)],
         [tokens_last(first_shape), tokens_last(third_shape)],
         [jax.ShapeDtypeStruct(first_shape, BF16), jax.ShapeDtypeStruct(third_shape, BF16)],
@@ -174,11 +174,53 @@
     )(third, teacher, w4_big, w4_big_t, *sums)
 
 
-def backward(turns, first, back, w2, w2_t, w3, sums, last):
+def slopes_back(order, first, back, w2, w2_t, w3):
     n_dev = back.shape[0]
     n_g, fan, tok = first.shape
     bw = w2.shape[2]
     n_q = w3.shape[0]
+    gq = n_g // n_q
+
+    def body(order_ref, first_ref, back_ref, w2_ref, w2t_ref, w3_ref, slope_ref, pre_ref, hid_ref):
+        @pl.loop(0, n_q, unroll=n_q)
+        def _(q):
+            held = back_ref[:, pl.ds(q * ROWS, ROWS), :].reshape(n_dev * ROWS, TILE)
+            both = []
+            for j in range(gq):
+                g = q * gq + j
+                pre = nn(w2t_ref[g], first_ref[g])
+                cdf = 0.5 * (1.0 + lax.erf(pre * SQRT_HALF))
+                hid_ref[q, j * bw : (j + 1) * bw, :] = (pre * cdf).astype(BF16)
+                rise = cdf + pre * jnp.exp(-0.5 * pre * pre) * INV_SQRT_2PI
+                back_hidden = nn(w3_ref[q, j * bw : (j + 1) * bw, :], held)
+                slope = (back_hidden * rise).astype(BF16)
+                pre_ref[g] = slope
+                both.append(nn(w2_ref[g], slope).reshape(fan // SUB, SUB, TILE))
+                if j % 2:
+                    at = pl.multiple_of((g - 1) * SUB, ROWS)
+                    pair = jnp.concatenate(both, axis=1).astype(BF16)
+                    slope_ref[:, pl.ds(at, ROWS), :] = pair
+                    both = []
+
+    shapes = [(fan // SUB, n_g * SUB, tok), (n_g, bw, tok), (n_q, gq * bw, tok)]
+    return call(
+        body,
+        tok // TILE,
+        [smem(), tokens_last(first.shape), tokens_last(back.shape)]
+        + [whole(a.shape) for a in (w2, w2_t, w3)],
+        [tokens_last(shape) for shape in shapes],
+        [jax.ShapeDtypeStruct(shape, BF16) for shape in shapes],
+        [],
+        2 * tok * 4 * n_g * bw * fan,
+        2 * (4 * first.size + back.size),
+    )(order, first, back, w2, w2_t, w3)
+
+
+def second_grads(turns, first, slope, hidden, back, sums, last):
+    n_dev = back.shape[0]
+    n_g, fan, tok = first.shape
+    bw = slope.shape[1]
+    n_q = hidden.shape[0]
     gq = n_g // n_q
     last_local = ROWS // gq
     n_e = n_dev * last_local
@@ -186,11 +228,9 @@
     out_shapes = [(n_g, fan + n_e, bw)] if last else sum_shapes
     n_out = len(out_shapes)
 
-    def body(*refs):
-        (turn_ref, first_ref, back_ref, w2_ref, w2t_ref, w3_ref), refs = refs[:6], refs[6:]
+    def body(turn_ref, first_ref, slope_ref, hid_ref, back_ref, *refs):
         start_refs, refs = refs[: len(sums)], refs[len(sums) :]
-        slope_ref, *out_refs = refs[: n_out + 1]
-        hid_ref, *acc_refs = refs[n_out + 1 :]
+        out_refs, acc_refs = refs[:n_out], refs[n_out:]
         acc_refs = acc_refs if last else out_refs
         acc2_ref, acc3_ref = acc_refs
         t = pl.program_id(0)
@@ -204,27 +244,13 @@
         @pl.loop(0, n_q, unroll=n_q)
         def _(q):
             held = back_ref[:, pl.ds(q * ROWS, ROWS), :].reshape(n_dev * ROWS, TILE)
-            both, slopes = [], []
-            for j in range(gq):
+            for j in range(0, gq, 2):
                 g = q * gq + j
-                pre = nn(w2t_ref[g], first_ref[g])
-                cdf = 0.5 * (1.0 + lax.erf(pre * SQRT_HALF))
-                hid_ref[j * bw : (j + 1) * bw, :] = (pre * cdf).astype(BF16)
-                rise = cdf + pre * jnp.exp(-0.5 * pre * pre) * INV_SQRT_2PI
-                back_hidden = nn(w3_ref[q, j * bw : (j + 1) * bw, :], held)
-                slope = (back_hidden * rise).astype(BF16)
-                slopes.append(slope)
-                both.append(nn(w2_ref[g], slope).reshape(fan // SUB, SUB, TILE))
-                if j % 2:
-                    left = first_ref[pl.ds(g - 1, 2)].reshape(2 * fan, TILE)
-                    prod = nt(left, jnp.concatenate(slopes, axis=0))
-                    acc2_ref[g - 1] += prod[:fan, :bw]
-                    acc2_ref[g] += prod[fan:, bw:]
-                    at = pl.multiple_of((g - 1) * SUB, ROWS)
-                    pair = jnp.concatenate(both, axis=1).astype(BF16)
-                    slope_ref[:, pl.ds(at, ROWS), :] = pair
-                    both, slopes = [], []
-            acc3_ref[q] += nt(hid_ref[...], held)
+                left = first_ref[pl.ds(g, 2)].reshape(2 * fan, TILE)
+                prod = nt(left, slope_ref[pl.ds(g, 2)].reshape(2 * bw, TILE))
+                acc2_ref[g] += prod[:fan, :bw]
+                acc2_ref[g + 1] += prod[fan:, bw:]
+            acc3_ref[q] += nt(hid_ref[q], held)
 
         @pl.when(t == pl.num_programs(0) - 1 if last else False)
         def _():
@@ -249,23 +275,21 @@
                         preferred_element_type=F32,
                     )
 
-    slope_shape = (fan // SUB, n_g * SUB, tok)
     return call(
         body,
         tok // TILE,
-        [smem(), tokens_last(first.shape), tokens_last(back.shape)]
-        + [whole(a.shape) for a in (w2, w2_t, w3, *sums)],
-        [tokens_last(slope_shape)] + [whole(shape) for shape in out_shapes],
-        [jax.ShapeDtypeStruct(slope_shape, BF16)]
-        + [jax.ShapeDtypeStruct(shape, F32) for shape in out_shapes],
-        [pltpu.VMEM((gq * bw, TILE), BF16)]
-        + [pltpu.VMEM(shape, F32) for shape in sum_shapes if last],
-        2 * tok * 6 * n_g * bw * fan,
-        2 * (2 * first.size + back.size),
-    )(turns, first, back, w2, w2_t, w3, *sums)
-
-
-def first_grad(pieces, order, row, turns, slope, n_g, in_width, held_sum, last):
+        [smem()]
+        + [tokens_last(a.shape) for a in (first, slope, hidden, back)]
+        + [whole(a.shape) for a in sums],
+        [whole(shape) for shape in out_shapes],
+        [jax.ShapeDtypeStruct(shape, F32) for shape in out_shapes],
+        [pltpu.VMEM(shape, F32) for shape in sum_shapes if last],
+        2 * tok * 2 * n_g * bw * fan,
+        2 * (3 * first.size + back.size),
+    )(turns, first, slope, hidden, back, *sums)
+
+
+def first_grad(pieces, order, turns, slope, n_g, in_width, held_sum, last):
     n_piece, rows, tok = slope.shape
     depth1 = pieces[0].shape[1]
     n_a = depth1 // in_width
@@ -306,7 +330,7 @@
     return call(
         body,
         tok // TILE,
-        [piece_spec(p.shape, row) for p in pieces]
+        [piece_spec(p.shape) for p in pieces]
         + [smem(), smem(), tokens_last(slope.shape)]
         + [whole(a.shape) for a in sums],
         whole(out_shape),
@@ -428,18 +452,20 @@
     return [parts[k] for k in range(4)]
 
 
-def gather_pieces(x, hold):
+def gather_pieces(x, before, hold):
+    x = follow(x, before)
     half = x.shape[1] // 2
     low, high = x[:, :half], x[:, half:]
     one = [turn(p, "blk", 2) for p in (low, high)]
     two = [turn(p, "blk", 4) for p in (low, high)]
-    one, two = follow((one, two), hold)
+    near = [turn(p, "blk", 1) for p in (low, high)]
+    one, two = follow((one, two), near, hold)
     both = [turn(one[0], "blk", 4), turn(two[1], "blk", 2)]
-    pieces = []
-    for group in ((low, high), one, two, both):
+    pieces = [low, high] + near
+    for group in (one, two):
         pieces.extend(group)
         pieces.extend(turn(p, "blk", 1) for p in group)
-    return pieces
+    return pieces + both
 
 
 def shards(cuts, student_in, teacher_out, w_first, w_second, w_third, w_fourth):
@@ -482,21 +508,34 @@
     w1 = follow(w1, w3_t, w4_big, w4_t)
 
     order = jnp.arange(n_piece, dtype=jnp.int32)
-    if n_dev == 8 and first_local == 2 * n_a:
+    paired = n_dev == 8 and first_local == 2 * n_a
+    if paired:
         order = order ^ (2 * lax.axis_index("blk")).astype(jnp.int32)
-        pieces = gather_pieces(student_in, (w1, w3_big, w3_t, w4_big, w4_t))
-    else:
-        x_all = lax.all_gather(student_in, "blk", axis=0)
-        pieces = [p for d in range(n_dev) for p in jnp.split(x_all[d], n_piece // n_dev, axis=1)]
-
-    firsts, thirds, backs, slopes, own_rest = [], [], [], [], []
+    gathered = []
+    prepared = (w1, w3_big, w3_t, w4_big, w4_t)
+
+    def do_gather(c):
+        x = student_in[bounds[c][0] : bounds[c][1]]
+        if paired:
+            gathered.append(gather_pieces(x, gathered[-1:], done if c else prepared))
+            return
+        x_all = lax.all_gather(x, "blk", axis=0)
+        each = n_piece // n_dev
+        gathered.append([p for d in range(n_dev) for p in jnp.split(x_all[d], each, axis=1)])
+
+    firsts, thirds, backs, slopes = [], [], [], []
     sums = ()
     grad_four = part_one = None
     done = ()
 
+    def do_last_pieces(c):
+        if paired:
+            both = follow(gathered[c][-2:], done)
+            gathered[c] = gathered[c][:-2] + both + [turn(p, "blk", 1) for p in both]
+
     def do_forward(c):
         nonlocal done
-        first, third = forward(pieces, follow(order, done), bounds[c], w1, w2_t, w3_t, n_dev)
+        first, third = forward(gathered[c], follow(order, done), w1, w2_t, w3_t, n_dev)
         firsts.append(first)
         thirds.append(swap(third))
         done = third
@@ -510,41 +549,45 @@
         backs.append(swap(back))
         done = back
 
-    def do_backward(c):
+    def do_slopes(c):
+        nonlocal done
+        slope, *kept = slopes_back(
+            follow(order, done), firsts[c], backs[c], w_second, w2_t, w3_big
+        )
+        slopes.append((slope, *kept))
+        done = slope
+
+    def do_second_grads(c):
         nonlocal done, sums
-        slope, *sums = backward(
-            follow(turns, done), firsts[c], backs[c], w_second, w2_t, w3_big, sums, c == n_chunks - 1
+        _, *kept = slopes[c]
+        sums = second_grads(
+            follow(turns, done), firsts[c], *kept, backs[c], sums, c == n_chunks - 1
         )
-        slopes.append(slope)
-        done = slope
+        done = sums
 
     def do_first_grad(c):
         nonlocal done, part_one, grad_four
         last = c == n_chunks - 1
         part_one = first_grad(
-            pieces, order, bounds[c][0], follow(turns, done), slopes[c], n_g, in_width, part_one, last
+            gathered[c], order, follow(turns, done), slopes[c][0], n_g, in_width, part_one, last
         )
         done = part_one
 
-    ring_state = {}
-
-    def do_ring(c):
-        nonlocal done
+    one_state = {}
+
+    def do_ring_one(c):
         if not ring:
             return
         if c == 0:
-            rest = sums[0].reshape(4, 2, n_g // 8, *sums[0].shape[1:])
-            ring_state["parts"] = [rest[:, h] for h in range(2)]
-            ring_state["got"] = [ring_send(rest[:, h], SIDES[h][0]) for h in range(2)]
+            one = part_one.reshape(4, 2, n_dev, spread, n_g, in_width)
+            one_state["parts"] = [one[:, h] for h in range(2)]
+            one_state["got"] = [ring_send(one[:, h], SIDES[h][0]) for h in range(2)]
             return
-        got = follow(ring_state["got"], done)
-        if c == 1:
-            halves = [ring_half(ring_state["parts"][h], got[h], SIDES[h][1]) for h in range(2)]
-            ring_state["mine"], ring_state["got"] = zip(*halves)
-            done = (done, ring_state["mine"])
-            return
-        pairs = zip(ring_state["mine"], got)
-        own_rest.extend((mine + part.astype(F32)).astype(BF16) for mine, part in pairs)
+        got = follow(one_state["got"], done)
+        one_state["own"] = []
+        for h in range(2):
+            mine, part = ring_half(one_state["parts"][h], got[h], SIDES[h][1])
+            one_state["own"].append((mine + part.astype(F32)).astype(BF16))
 
     four = {}
 
@@ -578,11 +621,14 @@
             grad_four = jnp.take(parts, rank, axis=0).reshape(four["shape"]).astype(F32)
 
     steps = {
+        "g": do_gather,
+        "h": do_last_pieces,
         "q": do_ring_four,
-        "r": do_ring,
+        "r": do_ring_one,
         "f": do_forward,
         "m": do_middle,
-        "b": do_backward,
+        "s": do_slopes,
+        "d": do_second_grads,
         "x": do_first_grad,
     }
     for step in PLAN:
@@ -597,11 +643,13 @@
         return (grad_one, grad_two, grad_three.transpose(0, 2, 1), grad_four.astype(F32))
 
     me = me_tok.reshape(1)
-    rest_halves = [ring_gather(own_rest[h], *SIDES[h]) for h in range(2)]
+    own = swap(jnp.stack(one_state["own"], axis=1))
+    rest = rest.reshape(4, 2, n_g // 8, *rest.shape[1:])
+    rest_halves = []
+    for h in range(2):
+        mine = ring_scatter(rest[:, h], *SIDES[h]).astype(BF16)
+        rest_halves.append(ring_gather(mine, *SIDES[h]))
     grad_two, grad_three = unpack_ring_rest(rest_halves, me, fan)
-    one = part_one.reshape(4, 2, n_dev, spread, n_g, in_width)
-    own = [ring_scatter(one[:, h], *SIDES[h]).astype(BF16) for h in range(2)]
-    own = swap(jnp.stack(own, axis=1))
     one_halves = [ring_gather(own[:, h], *SIDES[h]) for h in range(2)]
     grad_one = unpack_ring_first(one_halves, me, spread)
     return (grad_one, grad_two, grad_three.transpose(0, 2, 1), grad_four)

time: 459 us -> 451 us (0.983); the launches traced: 455 us -> 442 us
  waiting for transfers between devices: 174 us -> 127 us
  Pallas kernels: 157 us -> 172 us
  starting transfers between devices: 76.1 us -> 90.2 us
    all_to_all x6, waiting for transfers between devices: 94.8 us -> 46.6 us  [swap(): return lax.all_to_all(x, 'blk', split_axis=0, concat_axis=0, tiled=True)]
    ppermute x34 -> x48, starting transfers between devices: 42 us -> 65.5 us  [turn(): return lax.ppermute(x, axis, [(i, i ^ bits) for i in range(n)])]
    pallas_call x6 -> x8, Pallas kernels: 123 us -> 138 us  [the longest x2 53.6 us: slopes_back(): call(body, tok // TILE, [smem(), tokens_last(first.shape), tokens_last(ba...]
    all_to_all x6, starting transfers between devices: 34.2 us -> 24.7 us  [swap(): return lax.all_to_all(x, 'blk', split_axis=0, concat_axis=0, tiled=True)]
    ppermute x34 -> x48, waiting for transfers between devices: 79.3 us -> 80.9 us  [turn(): return lax.ppermute(x, axis, [(i, i ^ bits) for i in range(n)])]
  transfers between devices with their start and end apart: 40 -> 54, of which waited for: 18 -> 22; matrix products, arithmetic and copies ran while one was open for 9% -> 10% of each run, Pallas kernels for 31% -> 35%
where the time goes in v2:
time: 451 us; the launch traced here: 442 us
  Pallas kernels  172 us (38%)
  waiting for transfers between devices  127 us (28%)
  starting transfers between devices  90.2 us (20%)
  local copies, waits for them, and re-layouts  31.1 us (7%)
  other arithmetic  19.5 us (4%)
    ppermute x48, waiting for transfers between devices, turn(): return lax.ppermute(x, axis, [(i, i ^ bits) for i in range(n)])  80.9 us
    ppermute x48, starting transfers between devices, turn(): return lax.ppermute(x, axis, [(i, i ^ bits) for i in range(n)])  65.5 us
    pallas_call x2, Pallas kernels, slopes_back(): call(body, tok // TILE, [smem(), tokens_last(first.shape), tokens_last(ba...  53.6 us
    all_to_all x6, waiting for transfers between devices, swap(): return lax.all_to_all(x, 'blk', split_axis=0, concat_axis=0, tiled=True)  46.6 us
    pallas_call x2, Pallas kernels, forward(): call(body, tok // TILE, [piece_spec(p.shape) for p in pieces] + [smem(),...  32.5 us
    pallas_call x2, Pallas kernels, second_grads(): call(body, tok // TILE, [smem()] + [tokens_last(a.shape) for a in (first,...  29.7 us
    pallas_call x2, Pallas kernels, middle(): call(body, tok // TILE, [tokens_last(third.shape), pl.BlockSpec((TILE, co...  27.9 us
    all_to_all x6, starting transfers between devices, swap(): return lax.all_to_all(x, 'blk', split_axis=0, concat_axis=0, tiled=True)  24.7 us
  transfers between devices with their start and end apart: 54, of which 22 were waited for; matrix products, arithmetic and copies ran while one was open for 10% of the time, Pallas kernels for 35%

profile of v2, /device:TPU:0, one launch (start us, length us, event | category | flops | bytes accessed | tf_op | source)
XLA Modules:
  0.0 442.3 jit_solution(17862034326483518934)
XLA Ops:
  10.3 4.3 all-to-all-start
  25.4 28.8 %all-to-all-done = bf16[8,8,2,32,128]{4,3,2,1,0:T(8,128)(2,1)} async-done(((bf16[8,8,2,32,128]{4,3,2,1,0:T(8,128)(2,1)}), bf16[8,8,2,32,128]{4,3,2,1,0:T(8,128)(2,1)}, u32[]{:S(2)}, u32[]{:S(2)}) %all-to-all-start) | async-done | bytes 1048608 | tf_op jit(solution)/shard_map/all_to_all | solution.py:418
  60.0 14.9 %collective-permute-done.10.refs_12_ = bf16[768,512]{1,0:T(8,128)(2,1)S(1)} collective-permute-done((bf16[768,512]{1,0:T(8,128)(2,1)}, bf16[768,512]{1,0:T(8,128)(2,1)S(1)}, u32[]{:S(2)}, u32[]{:S(2)}) %collective-permute-start.10) | collective-permute-done | bytes 786464 | tf_op jit(solution)/shard_map/ppermute | solution.py:423
  90.1 14.6 %shard_map.102 = (bf16[32,128,768]{2,1,0:T(8,128)(2,1)}, bf16[8,128,768]{2,1,0:T(8,128)(2,1)}) custom-call(bf16[768,512]{1,0:T(8,128)(2,1)} %get-tuple-element.111.refs_0_, bf16[768,512]{1,0:T(8,128)(2,1)} %get-tuple-element.110.refs_1_, bf16[768,512]{1,0:T(8,128)(2,1)} %copy-done.12, bf16[768,512]{1,0:T(8,128)(2,1)} %collective-permute-done.1.refs_3_, ...), custom_call_target="tpu_custom_call" | custom-call | flops 4831838208 | bytes 19922944 | tf_op jit(solution)/shard_map/pallas_call | solution.py:105
  104.7 4.5 %all-to-all-start.1 = ((bf16[8,128,768]{2,1,0:T(8,128)(2,1)}), bf16[8,128,768]{2,1,0:T(8,128)(2,1)}, u32[]{:S(2)}, u32[]{:S(2)}) async-start(bf16[8,128,768]{2,1,0:T(8,128)(2,1)} %get-tuple-element.65), calls=%async_computation.1 | async-start | bytes 3145728 | tf_op jit(solution)/shard_map/all_to_all | solution.py:418
  111.9 22.5 %collective-permute-done.17.refs_5_ = bf16[1024,512]{1,0:T(8,128)(2,1)} collective-permute-done((bf16[1024,512]{1,0:T(8,128)(2,1)S(1)}, bf16[1024,512]{1,0:T(8,128)(2,1)}, u32[]{:S(2)}, u32[]{:S(2)}) %collective-permute-start.17) | collective-permute-done | bytes 1048608 | tf_op jit(solution)/shard_map/ppermute | solution.py:423
  138.1 4.7 %collective-permute-start.25 = (bf16[1024,512]{1,0:T(8,128)(2,1)}, bf16[1024,512]{1,0:T(8,128)(2,1)}, u32[]{:S(2)}, u32[]{:S(2)}) collective-permute-start(bf16[1024,512]{1,0:T(8,128)(2,1)} %collective-permute-done.19.refs_9_), channel_id=1, source_target_pairs={{0,2},{1,3},{2,0},{3,1},{4,6},{5,7},{6,4},{7,5},{8,10},{9,11},{10,... | collective-permute-start | bytes 3145736 | tf_op jit(solution)/shard_map/ppermute | solution.py:423
  143.3 10.2 %all-to-all-done.1.third_ref = bf16[8,128,768]{2,1,0:T(8,128)(2,1)} async-done(((bf16[8,128,768]{2,1,0:T(8,128)(2,1)}), bf16[8,128,768]{2,1,0:T(8,128)(2,1)}, u32[]{:S(2)}, u32[]{:S(2)}) %all-to-all-start.1) | async-done | bytes 1572896 | tf_op jit(solution)/shard_map/all_to_all | solution.py:418
  153.5 12.4 %shard_map.103 = (bf16[8,128,768]{2,1,0:T(8,128)(2,1)}, f32[2,1024,128]{2,1,0:T(8,128)}) custom-call(bf16[8,128,768]{2,1,0:T(8,128)(2,1)} %all-to-all-done.1.third_ref, bf16[1792,1024]{1,0:T(8,128)(2,1)} %teach_ref.3, bf16[1024,1024]{1,0:T(8,128)(2,1)} %bitcast.196, bf16[1024,1024]{1,0:T(8,128)(2,1)} %bitcast.200), custom_call_target="tpu_custom_call" | custom-call | flops 4831838208 | bytes 8912896 | tf_op jit(solution)/shard_map/pallas_call | solution.py:159
  165.9 9.0 %collective-permute-done.24.refs_12_ = bf16[1024,512]{1,0:T(8,128)(2,1)S(1)} collective-permute-done((bf16[1024,512]{1,0:T(8,128)(2,1)}, bf16[1024,512]{1,0:T(8,128)(2,1)S(1)}, u32[]{:S(2)}, u32[]{:S(2)}) %collective-permute-start.24) | collective-permute-done | bytes 1048608 | tf_op jit(solution)/shard_map/ppermute | solution.py:423
  180.9 17.9 %shard_map.104 = (bf16[32,128,1024]{2,1,0:T(8,128)(2,1)}, bf16[8,128,1024]{2,1,0:T(8,128)(2,1)}) custom-call(bf16[1024,512]{1,0:T(8,128)(2,1)} %copy-done.5, bf16[1024,512]{1,0:T(8,128)(2,1)} %copy-done.4, bf16[1024,512]{1,0:T(8,128)(2,1)} %collective-permute-done.14.refs_2_, bf16[1024,512]{1,0:T(8,128)(2,1)} %collective-permute-done.15.refs_3_, ...), custom_call_target="tpu_custom_call" | custom-call | flops 6442450944 | bytes 26214400 | tf_op jit(solution)/shard_map/pallas_call | solution.py:105
  202.2 4.3 all-to-all-start.2
  206.5 23.7 %shard_map.105 = (bf16[16,256,768]{2,1,0:T(8,128)(2,1)}, bf16[32,128,768]{2,1,0:T(8,128)(2,1)}, bf16[8,512,768]{2,1,0:T(8,128)(2,1)}) custom-call(s32[16]{0:T(128)} %iota_xor_fusion.refs_16_.order_ref, bf16[32,128,768]{2,1,0:T(8,128)(2,1)} %get-tuple-element.77.first_ref, bf16[8,128,768]{2,1,0:T(8,128)(2,1)} %copy-done.3, bf16[32,128,128]{2,1,0:T(8,128)(2,1)} %w2_ref.3, ...), custom_call_target="tpu_custom_call" | custom-call | flops 3221225472 | bytes 26738688 | tf_op jit(solution)/shard_map/pallas_call | solution.py:206
  233.2 15.5 %shard_map.106 = (bf16[8,128,1024]{2,1,0:T(8,128)(2,1)}, f32[4,256,256]{2,1,0:T(8,128)}) custom-call(bf16[8,128,1024]{2,1,0:T(8,128)(2,1)} %all-to-all-done.2.third_ref, bf16[1792,1024]{1,0:T(8,128)(2,1)} %teach_ref.3, bf16[1024,1024]{1,0:T(8,128)(2,1)} %bitcast.197, bf16[1024,1024]{1,0:T(8,128)(2,1)} %bitcast.201, f32[2,1024,128]{2,1,0:T(8,128)} %get-tuple-element.80.refs_0_), custom_call_target="tpu_custom_call" | custom-call | flops 6442450944 | bytes 10485760 | tf_op jit(solution)/shard_map/pallas_call | solution.py:159
  248.7 4.0 all-to-all-start.4
  257.9 10.8 %shard_map.107 = (f32[32,128,128]{2,1,0:T(8,128)}, f32[8,512,128]{2,1,0:T(8,128)}) custom-call(s32[2]{0:T(128)} %broadcast_multiply_fusion.2.turn_ref.refs_17_, bf16[32,128,768]{2,1,0:T(8,128)(2,1)} %get-tuple-element.77.first_ref, bf16[32,128,768]{2,1,0:T(8,128)(2,1)} %get-tuple-element.83.slope_ref, bf16[8,512,768]{2,1,0:T(8,128)(2,1)} %get-tuple-element.84.hid_ref, ...), custom_call_target="tpu_custom_call" | custom-call | flops 1610612736 | bytes 20447232 | tf_op jit(solution)/shard_map/pallas_call | solution.py:278
  268.8 9.9 %shard_map.108.refs_19_ = f32[16,256,128]{2,1,0:T(8,128)} custom-call(bf16[768,512]{1,0:T(8,128)(2,1)} %get-tuple-element.111.refs_0_, bf16[768,512]{1,0:T(8,128)(2,1)} %get-tuple-element.110.refs_1_, bf16[768,512]{1,0:T(8,128)(2,1)} %copy-done.12, bf16[768,512]{1,0:T(8,128)(2,1)} %collective-permute-done.1.refs_3_, ...), custom_call_target="tpu_custom_call" | custom-call | flops 3221225472 | bytes 18874368 | tf_op jit(solution)/shard_map/pallas_call | solution.py:330
  282.5 29.9 %shard_map.109 = (bf16[16,256,1024]{2,1,0:T(8,128)(2,1)}, bf16[32,128,1024]{2,1,0:T(8,128)(2,1)}, bf16[8,512,1024]{2,1,0:T(8,128)(2,1)}) custom-call(s32[16]{0:T(128)} %iota_xor_fusion.refs_16_.order_ref, bf16[32,128,1024]{2,1,0:T(8,128)(2,1)} %get-tuple-element.91.first_ref, bf16[8,128,1024]{2,1,0:T(8,128)(2,1)} %copy-done.1, bf16[32,128,128]{2,1,0:T(8,128)(2,1)} %w2_ref.3, ...), custom_call_target="tpu_custom_call" | custom-call | flops 4294967296 | bytes 35651584 | tf_op jit(solution)/shard_map/pallas_call | solution.py:206
  314.1 12.8 %shard_map.110 = f32[8,8,2,32,128]{4,3,2,1,0:T(8,128)} custom-call(bf16[1024,512]{1,0:T(8,128)(2,1)} %copy-done.5, bf16[1024,512]{1,0:T(8,128)(2,1)} %copy-done.4, bf16[1024,512]{1,0:T(8,128)(2,1)} %collective-permute-done.14.refs_2_, bf16[1024,512]{1,0:T(8,128)(2,1)} %collective-permute-done.15.refs_3_, bf16[1024,512]{1,0:T(8,128)(2,1)} %collective-permute-done.16.refs_4_, ...), custom_call_target="tpu_custom_call" | custom-call | flops 4294967296 | bytes 25165824 | tf_op jit(solution)/shard_map/pallas_call | solution.py:330
  333.3 18.9 %shard_map.111 = f32[32,160,128]{2,1,0:T(8,128)} custom-call(s32[2]{0:T(128)} %broadcast_multiply_fusion.2.turn_ref.refs_17_, bf16[32,128,1024]{2,1,0:T(8,128)(2,1)} %get-tuple-element.91.first_ref, bf16[32,128,1024]{2,1,0:T(8,128)(2,1)} %get-tuple-element.97.slope_ref, bf16[8,512,1024]{2,1,0:T(8,128)(2,1)} %get-tuple-element.98.hid_ref, ...), custom_call_target="tpu_custom_call" | custom-call | flops 2147483648 | bytes 27262976 | tf_op jit(solution)/shard_map/pallas_call | solution.py:278
  369.2 7.8 %collective-permute-done.43 = bf16[2,4,160,128]{3,2,1,0:T(8,128)(2,1)} collective-permute-done((bf16[2,4,160,128]{3,2,1,0:T(8,128)(2,1)}, bf16[2,4,160,128]{3,2,1,0:T(8,128)(2,1)}, u32[]{:S(2)}, u32[]{:S(2)}) %collective-permute-start.43) | collective-permute-done | bytes 327712 | tf_op jit(solution)/shard_map/ppermute | solution.py:423
  380.3 4.0 all-to-all-start.5
  403.2 10.5 %collective-permute-done.41.refs_3_ = bf16[4,160,128]{2,1,0:T(8,128)(2,1)S(1)} collective-permute-done((bf16[4,160,128]{2,1,0:T(8,128)(2,1)S(1)}, bf16[4,160,128]{2,1,0:T(8,128)(2,1)S(1)}, u32[]{:S(2)}, u32[]{:S(2)}) %collective-permute-start.41) | collective-permute-done | bytes 163872 | tf_op jit(solution)/shard_map/ppermute | solution.py:423
  413.7 16.3 %collective-permute-start.42 = (bf16[2,4,160,128]{3,2,1,0:T(8,128)(2,1)S(1)}, bf16[2,4,160,128]{3,2,1,0:T(8,128)(2,1)S(1)}, u32[]{:S(2)}, u32[]{:S(2)}) collective-permute-start(bf16[2,4,160,128]{3,2,1,0:T(8,128)(2,1)S(1)} %pad_maximum_fusion.2), channel_id=1, source_target_pairs={{0,8},{8,0},{16,24},{24,16},{1,9},{9,1},{17,25},{25,17},{2,10},{10... | collective-permute-start | bytes 983048 | tf_op jit(solution)/shard_map/ppermute | solution.py:423
  (220 shorter events, 128.5 us)
Async XLA Ops:
  3.7 53.7 %collective-permute-start.2 = (bf16[768,512]{1,0:T(8,128)(2,1)}, bf16[768,512]{1,0:T(8,128)(2,1)}, u32[]{:S(2)}, u32[]{:S(2)}) collective-permute-start(bf16[768,512]{1,0:T(8,128)(2,1)} %get-tuple-element.111.refs_0_), channel_id=1, source_target_pairs={{0,2},{1,3},{2,0},{3,1},{4,6},{5,7},{6,4},{7,5},{8,10},{9,11},{10,... | collective-permute-start | bytes 2359304 | tf_op jit(solution)/shard_map/ppermute | solution.py:423
  6.2 51.2 %collective-permute-start.1 = (bf16[768,512]{1,0:T(8,128)(2,1)}, bf16[768,512]{1,0:T(8,128)(2,1)}, u32[]{:S(2)}, u32[]{:S(2)}) collective-permute-start(bf16[768,512]{1,0:T(8,128)(2,1)} %get-tuple-element.110.refs_1_), channel_id=1, source_target_pairs={{0,1},{1,0},{2,3},{3,2},{4,5},{5,4},{6,7},{7,6},{8,9},{9,8},{10,11... | collective-permute-start | bytes 2359304 | tf_op jit(solution)/shard_map/ppermute | solution.py:423
  6.5 51.0 %collective-permute-start.3 = (bf16[768,512]{1,0:T(8,128)(2,1)}, bf16[768,512]{1,0:T(8,128)(2,1)}, u32[]{:S(2)}, u32[]{:S(2)}) collective-permute-start(bf16[768,512]{1,0:T(8,128)(2,1)} %get-tuple-element.110.refs_1_), channel_id=1, source_target_pairs={{0,2},{1,3},{2,0},{3,1},{4,6},{5,7},{6,4},{7,5},{8,10},{9,11},{10,... | collective-permute-start | bytes 2359304 | tf_op jit(solution)/shard_map/ppermute | solution.py:423
  6.7 50.7 %collective-permute-start.4 = (bf16[768,512]{1,0:T(8,128)(2,1)}, bf16[768,512]{1,0:T(8,128)(2,1)}, u32[]{:S(2)}, u32[]{:S(2)}) collective-permute-start(bf16[768,512]{1,0:T(8,128)(2,1)} %get-tuple-element.111.refs_0_), channel_id=1, source_target_pairs={{0,4},{1,5},{2,6},{3,7},{4,0},{5,1},{6,2},{7,3},{8,12},{9,13},{10,... | collective-permute-start | bytes 2359304 | tf_op jit(solution)/shard_map/ppermute | solution.py:423
  10.3 43.9 %all-to-all-start = ((bf16[8,8,2,32,128]{4,3,2,1,0:T(8,128)(2,1)}), bf16[8,8,2,32,128]{4,3,2,1,0:T(8,128)(2,1)}, u32[]{:S(2)}, u32[]{:S(2)}) async-start(bf16[8,8,2,32,128]{4,3,2,1,0:T(8,128)(2,1)} %copy.32), calls=%async_computation | async-start | bytes 2097152 | tf_op jit(solution)/shard_map/all_to_all | solution.py:418
  15.1 42.3 %collective-permute-start.5 = (bf16[768,512]{1,0:T(8,128)(2,1)}, bf16[768,512]{1,0:T(8,128)(2,1)}, u32[]{:S(2)}, u32[]{:S(2)}) collective-permute-start(bf16[768,512]{1,0:T(8,128)(2,1)} %get-tuple-element.110.refs_1_), channel_id=1, source_target_pairs={{0,4},{1,5},{2,6},{3,7},{4,0},{5,1},{6,2},{7,3},{8,12},{9,13},{10,... | collective-permute-start | bytes 2359304 | tf_op jit(solution)/shard_map/ppermute | solution.py:423
  85.8 26.1 %collective-permute-start.16 = (bf16[1024,512]{1,0:T(8,128)(2,1)S(1)}, bf16[1024,512]{1,0:T(8,128)(2,1)}, u32[]{:S(2)}, u32[]{:S(2)}) collective-permute-start(bf16[1024,512]{1,0:T(8,128)(2,1)S(1)} %get-tuple-element.109.refs_0_), channel_id=1, source_target_pairs={{0,2},{1,3},{2,0},{3,1},{4,6},{5,7},{6,4},{7,5},{8,10},{9,11},{10,... | collective-permute-start | bytes 3145736 | tf_op jit(solution)/shard_map/ppermute | solution.py:423
  86.6 47.8 %collective-permute-start.17 = (bf16[1024,512]{1,0:T(8,128)(2,1)S(1)}, bf16[1024,512]{1,0:T(8,128)(2,1)}, u32[]{:S(2)}, u32[]{:S(2)}) collective-permute-start(bf16[1024,512]{1,0:T(8,128)(2,1)S(1)} %get-tuple-element.108.refs_1_), channel_id=1, source_target_pairs={{0,2},{1,3},{2,0},{3,1},{4,6},{5,7},{6,4},{7,5},{8,10},{9,11},{10,... | collective-permute-start | bytes 3145736 | tf_op jit(solution)/shard_map/ppermute | solution.py:423
  88.1 46.3 %collective-permute-start.18 = (bf16[1024,512]{1,0:T(8,128)(2,1)S(1)}, bf16[1024,512]{1,0:T(8,128)(2,1)}, u32[]{:S(2)}, u32[]{:S(2)}) collective-permute-start(bf16[1024,512]{1,0:T(8,128)(2,1)S(1)} %get-tuple-element.109.refs_0_), channel_id=1, source_target_pairs={{0,4},{1,5},{2,6},{3,7},{4,0},{5,1},{6,2},{7,3},{8,12},{9,13},{10,... | collective-permute-start | bytes 3145736 | tf_op jit(solution)/shard_map/ppermute | solution.py:423
  89.5 47.2 %collective-permute-start.19 = (bf16[1024,512]{1,0:T(8,128)(2,1)S(1)}, bf16[1024,512]{1,0:T(8,128)(2,1)}, u32[]{:S(2)}, u32[]{:S(2)}) collective-permute-start(bf16[1024,512]{1,0:T(8,128)(2,1)S(1)} %get-tuple-element.108.refs_1_), channel_id=1, source_target_pairs={{0,4},{1,5},{2,6},{3,7},{4,0},{5,1},{6,2},{7,3},{8,12},{9,13},{10,... | collective-permute-start | bytes 3145736 | tf_op jit(solution)/shard_map/ppermute | solution.py:423
  104.7 48.8 %all-to-all-start.1 = ((bf16[8,128,768]{2,1,0:T(8,128)(2,1)}), bf16[8,128,768]{2,1,0:T(8,128)(2,1)}, u32[]{:S(2)}, u32[]{:S(2)}) async-start(bf16[8,128,768]{2,1,0:T(8,128)(2,1)} %get-tuple-element.65), calls=%async_computation.1 | async-start | bytes 3145728 | tf_op jit(solution)/shard_map/all_to_all | solution.py:418
  136.7 38.3 %collective-permute-start.24 = (bf16[1024,512]{1,0:T(8,128)(2,1)}, bf16[1024,512]{1,0:T(8,128)(2,1)S(1)}, u32[]{:S(2)}, u32[]{:S(2)}) collective-permute-start(bf16[1024,512]{1,0:T(8,128)(2,1)} %collective-permute-done.16.refs_4_), channel_id=1, source_target_pairs={{0,4},{1,5},{2,6},{3,7},{4,0},{5,1},{6,2},{7,3},{8,12},{9,13},{10,... | collective-permute-start | bytes 3145736 | tf_op jit(solution)/shard_map/ppermute | solution.py:423
  138.1 36.9 %collective-permute-start.25 = (bf16[1024,512]{1,0:T(8,128)(2,1)}, bf16[1024,512]{1,0:T(8,128)(2,1)}, u32[]{:S(2)}, u32[]{:S(2)}) collective-permute-start(bf16[1024,512]{1,0:T(8,128)(2,1)} %collective-permute-done.19.refs_9_), channel_id=1, source_target_pairs={{0,2},{1,3},{2,0},{3,1},{4,6},{5,7},{6,4},{7,5},{8,10},{9,11},{10,... | collective-permute-start | bytes 3145736 | tf_op jit(solution)/shard_map/ppermute | solution.py:423
  142.8 32.6 %collective-permute-start.20 = (bf16[1024,512]{1,0:T(8,128)(2,1)}, bf16[1024,512]{1,0:T(8,128)(2,1)S(1)}, u32[]{:S(2)}, u32[]{:S(2)}) collective-permute-start(bf16[1024,512]{1,0:T(8,128)(2,1)} %collective-permute-done.16.refs_4_), channel_id=1, source_target_pairs={{0,1},{1,0},{2,3},{3,2},{4,5},{5,4},{6,7},{7,6},{8,9},{9,8},{10,11... | collective-permute-start | bytes 3145736 | tf_op jit(solution)/shard_map/ppermute | solution.py:423
  142.8 37.3 %collective-permute-start.23 = (bf16[1024,512]{1,0:T(8,128)(2,1)}, bf16[1024,512]{1,0:T(8,128)(2,1)}, u32[]{:S(2)}, u32[]{:S(2)}) collective-permute-start(bf16[1024,512]{1,0:T(8,128)(2,1)} %collective-permute-done.19.refs_9_), channel_id=1, source_target_pairs={{0,1},{1,0},{2,3},{3,2},{4,5},{5,4},{6,7},{7,6},{8,9},{9,8},{10,11... | collective-permute-start | bytes 3145736 | tf_op jit(solution)/shard_map/ppermute | solution.py:423
  143.3 36.7 %collective-permute-start.21 = (bf16[1024,512]{1,0:T(8,128)(2,1)}, bf16[1024,512]{1,0:T(8,128)(2,1)}, u32[]{:S(2)}, u32[]{:S(2)}) collective-permute-start(bf16[1024,512]{1,0:T(8,128)(2,1)} %collective-permute-done.17.refs_5_), channel_id=1, source_target_pairs={{0,1},{1,0},{2,3},{3,2},{4,5},{5,4},{6,7},{7,6},{8,9},{9,8},{10,11... | collective-permute-start | bytes 3145736 | tf_op jit(solution)/shard_map/ppermute | solution.py:423
  202.2 31.0 %all-to-all-start.2 = ((bf16[8,128,1024]{2,1,0:T(8,128)(2,1)}), bf16[8,128,1024]{2,1,0:T(8,128)(2,1)}, u32[]{:S(2)}, u32[]{:S(2)}) async-start(bf16[8,128,1024]{2,1,0:T(8,128)(2,1)} %get-tuple-element.75), calls=%async_computation.2 | async-start | bytes 4194304 | tf_op jit(solution)/shard_map/all_to_all | solution.py:418
  248.7 32.5 %all-to-all-start.4 = ((bf16[8,128,1024]{2,1,0:T(8,128)(2,1)}), bf16[8,128,1024]{2,1,0:T(8,128)(2,1)S(1)}, u32[]{:S(2)}, u32[]{:S(2)}) async-start(bf16[8,128,1024]{2,1,0:T(8,128)(2,1)} %get-tuple-element.81), calls=%async_computation.4 | async-start | bytes 4194304 | tf_op jit(solution)/shard_map/all_to_all | solution.py:418
  278.6 33.7 %collective-permute-start.29 = (bf16[512,128]{1,0:T(8,128)(2,1)S(1)}, bf16[512,128]{1,0:T(8,128)(2,1)S(1)}, u32[]{:S(2)}, u32[]{:S(2)}) collective-permute-start(bf16[512,128]{1,0:T(8,128)(2,1)S(1)} %get-tuple-element.116), channel_id=1, source_target_pairs={{0,24},{8,16},{16,8},{24,0},{1,25},{9,17},{17,9},{25,1},{2,26},{10... | collective-permute-start | bytes 393224 | tf_op jit(solution)/shard_map/ppermute | solution.py:423
  331.3 29.3 %collective-permute-start.47 = (bf16[2,512,128]{2,1,0:T(8,128)(2,1)S(1)}, bf16[2,512,128]{2,1,0:T(8,128)(2,1)S(1)}, u32[]{:S(2)}, u32[]{:S(2)}) collective-permute-start(bf16[2,512,128]{2,1,0:T(8,128)(2,1)S(1)} %pad_maximum_fusion.7), channel_id=1, source_target_pairs={{0,8},{8,0},{16,24},{24,16},{1,9},{9,1},{17,25},{25,17},{2,10},{10... | collective-permute-start | bytes 786440 | tf_op jit(solution)/shard_map/ppermute | solution.py:423
  357.6 26.7 %collective-permute-start.39 = (bf16[2,4,160,128]{3,2,1,0:T(8,128)(2,1)}, bf16[2,4,160,128]{3,2,1,0:T(8,128)(2,1)}, u32[]{:S(2)}, u32[]{:S(2)}) collective-permute-start(bf16[2,4,160,128]{3,2,1,0:T(8,128)(2,1)} %pad_maximum_fusion.1), channel_id=1, source_target_pairs={{0,8},{8,0},{16,24},{24,16},{1,9},{9,1},{17,25},{25,17},{2,10},{10... | collective-permute-start | bytes 983048 | tf_op jit(solution)/shard_map/ppermute | solution.py:423
  394.7 35.2 %collective-permute-start.46 = (bf16[2,4,160,128]{3,2,1,0:T(8,128)(2,1)S(1)}, bf16[2,4,160,128]{3,2,1,0:T(8,128)(2,1)S(1)}, u32[]{:S(2)}, u32[]{:S(2)}) collective-permute-start(bf16[2,4,160,128]{3,2,1,0:T(8,128)(2,1)S(1)} %pad_maximum_fusion.4), channel_id=1, source_target_pairs={{0,24},{8,16},{16,8},{24,0},{1,25},{9,17},{17,9},{25,1},{2,26},{10... | collective-permute-start | bytes 983048 | tf_op jit(solution)/shard_map/ppermute | solution.py:423
  400.8 29.9 %collective-permute-start.38 = (bf16[2,8,2,32,128]{4,3,2,1,0:T(8,128)(2,1)S(1)}, bf16[2,8,2,32,128]{4,3,2,1,0:T(8,128)(2,1)S(1)}, u32[]{:S(2)}, u32[]{:S(2)}) collective-permute-start(bf16[2,8,2,32,128]{4,3,2,1,0:T(8,128)(2,1)S(1)} %pad_maximum_fusion.10), channel_id=1, source_target_pairs={{0,24},{8,16},{16,8},{24,0},{1,25},{9,17},{17,9},{25,1},{2,26},{10... | collective-permute-start | bytes 786440 | tf_op jit(solution)/shard_map/ppermute | solution.py:423
  403.1 28.4 %collective-permute-start.36 = (bf16[2,8,2,32,128]{4,3,2,1,0:T(8,128)(2,1)S(1)}, bf16[2,8,2,32,128]{4,3,2,1,0:T(8,128)(2,1)S(1)}, u32[]{:S(2)}, u32[]{:S(2)}) collective-permute-start(bf16[2,8,2,32,128]{4,3,2,1,0:T(8,128)(2,1)S(1)} %pad_maximum_fusion.9), channel_id=1, source_target_pairs={{0,8},{8,0},{16,24},{24,16},{1,9},{9,1},{17,25},{25,17},{2,10},{10... | collective-permute-start | bytes 786440 | tf_op jit(solution)/shard_map/ppermute | solution.py:423
  (61 other events, 774.8 us)

commit v3 on v2

--- a/solution.py
+++ b/solution.py
@@ -265,7 +265,7 @@
                 for j in range(gq):
                     g = q * gq + j
                     to = g ^ turn_g
-                    out_refs[0][to, :fan, :] = acc2_ref[g]
+                    out_refs[0][to, :fan, :] = acc2_ref[g].astype(BF16)
                     rows = jnp.where(lane == j, acc3_ref[q, j * bw : (j + 1) * bw, :], 0.0)
                     out_refs[0][to, fan:, :] = lax.dot_general(
                         pick,
@@ -273,7 +273,7 @@
                         (((1,), (1,)), ((), ())),
                         precision=lax.Precision.HIGHEST,
                         preferred_element_type=F32,
-                    )
+                    ).astype(BF16)
 
     return call(
         body,
@@ -282,7 +282,7 @@
         + [tokens_last(a.shape) for a in (first, slope, hidden, back)]
         + [whole(a.shape) for a in sums],
         [whole(shape) for shape in out_shapes],
-        [jax.ShapeDtypeStruct(shape, F32) for shape in out_shapes],
+        [jax.ShapeDtypeStruct(shape, BF16 if last else F32) for shape in out_shapes],
         [pltpu.VMEM(shape, F32) for shape in sum_shapes if last],
         2 * tok * 2 * n_g * bw * fan,
         2 * (3 * first.size + back.size),
@@ -325,7 +325,7 @@
                 for r in range(SUB):
                     a = p % 2 * n_a + r // spread
                     picked = acc_ref[p, pl.ds(r, n_g, stride=SUB), :]
-                    out_ref[a ^ turn_a, p // 2, r % spread] = picked
+                    out_ref[a ^ turn_a, p // 2, r % spread] = picked.astype(BF16)
 
     return call(
         body,
@@ -334,7 +334,7 @@
         + [smem(), smem(), tokens_last(slope.shape)]
         + [whole(a.shape) for a in sums],
         whole(out_shape),
-        jax.ShapeDtypeStruct(out_shape, F32),
+        jax.ShapeDtypeStruct(out_shape, BF16 if last else F32),
         [pltpu.VMEM(sum_shape, F32)] if last else [],
         2 * tok * n_piece * rows * depth1,
         2 * (n_piece * depth1 * tok + slope.size),

time: 451 us -> 447 us (level)
  starting transfers between devices: 90.2 us -> 100 us
  other arithmetic: 19.5 us -> 12.3 us
  waiting for transfers between devices: 127 us -> 121 us
    ppermute x48, starting transfers between devices: 65.5 us -> 75.5 us  [turn(): return lax.ppermute(x, axis, [(i, i ^ bits) for i in range(n)])]
    ppermute x48, waiting for transfers between devices: 80.9 us -> 74 us  [turn(): return lax.ppermute(x, axis, [(i, i ^ bits) for i in range(n)])]
  transfers between devices with their start and end apart: 54 -> 54, of which waited for: 22 -> 22; matrix products, arithmetic and copies ran while one was open for 10% -> 8% of each run, Pallas kernels for 35% -> 35%
where the time goes in v3:
time: 447 us; the launch traced here: 438 us
  Pallas kernels  172 us (38%)
  waiting for transfers between devices  121 us (27%)
  starting transfers between devices  100 us (22%)
  local copies, waits for them, and re-layouts  31.5 us (7%)
  other arithmetic  12.3 us (3%)
    ppermute x48, starting transfers between devices, turn(): return lax.ppermute(x, axis, [(i, i ^ bits) for i in range(n)])  75.5 us
    ppermute x48, waiting for transfers between devices, turn(): return lax.ppermute(x, axis, [(i, i ^ bits) for i in range(n)])  74 us
    pallas_call x2, Pallas kernels, slopes_back(): call(body, tok // TILE, [smem(), tokens_last(first.shape), tokens_last(ba...  53.6 us
    all_to_all x6, waiting for transfers between devices, swap(): return lax.all_to_all(x, 'blk', split_axis=0, concat_axis=0, tiled=True)  47.2 us
    pallas_call x2, Pallas kernels, forward(): call(body, tok // TILE, [piece_spec(p.shape) for p in pieces] + [smem(),...  32.5 us
    pallas_call x2, Pallas kernels, second_grads(): call(body, tok // TILE, [smem()] + [tokens_last(a.shape) for a in (first,...  29.3 us
    pallas_call x2, Pallas kernels, middle(): call(body, tok // TILE, [tokens_last(third.shape), pl.BlockSpec((TILE, co...  27.8 us
    all_to_all x6, starting transfers between devices, swap(): return lax.all_to_all(x, 'blk', split_axis=0, concat_axis=0, tiled=True)  24.4 us
  transfers between devices with their start and end apart: 54, of which 22 were waited for; matrix products, arithmetic and copies ran while one was open for 8% of the time, Pallas kernels for 35%

profile of v3, /device:TPU:0, one launch (start us, length us, event | category | flops | bytes accessed | tf_op | source)
XLA Modules:
  0.0 438.2 jit_solution(4778431785295000630)
XLA Ops:
  10.3 4.2 all-to-all-start
  25.4 28.8 %all-to-all-done = bf16[8,8,2,32,128]{4,3,2,1,0:T(8,128)(2,1)} async-done(((bf16[8,8,2,32,128]{4,3,2,1,0:T(8,128)(2,1)}), bf16[8,8,2,32,128]{4,3,2,1,0:T(8,128)(2,1)}, u32[]{:S(2)}, u32[]{:S(2)}) %all-to-all-start) | async-done | bytes 1048608 | tf_op jit(solution)/shard_map/all_to_all | solution.py:418
  60.1 14.9 %collective-permute-done.10.refs_12_ = bf16[768,512]{1,0:T(8,128)(2,1)S(1)} collective-permute-done((bf16[768,512]{1,0:T(8,128)(2,1)}, bf16[768,512]{1,0:T(8,128)(2,1)S(1)}, u32[]{:S(2)}, u32[]{:S(2)}) %collective-permute-start.10) | collective-permute-done | bytes 786464 | tf_op jit(solution)/shard_map/ppermute | solution.py:423
  90.1 14.6 %shard_map.102 = (bf16[32,128,768]{2,1,0:T(8,128)(2,1)}, bf16[8,128,768]{2,1,0:T(8,128)(2,1)}) custom-call(bf16[768,512]{1,0:T(8,128)(2,1)} %get-tuple-element.107.refs_0_, bf16[768,512]{1,0:T(8,128)(2,1)} %get-tuple-element.106.refs_1_, bf16[768,512]{1,0:T(8,128)(2,1)} %copy-done.13, bf16[768,512]{1,0:T(8,128)(2,1)} %collective-permute-done.1.refs_3_, ...), custom_call_target="tpu_custom_call" | custom-call | flops 4831838208 | bytes 19922944 | tf_op jit(solution)/shard_map/pallas_call | solution.py:105
  104.7 4.5 %all-to-all-start.1 = ((bf16[8,128,768]{2,1,0:T(8,128)(2,1)}), bf16[8,128,768]{2,1,0:T(8,128)(2,1)}, u32[]{:S(2)}, u32[]{:S(2)}) async-start(bf16[8,128,768]{2,1,0:T(8,128)(2,1)} %get-tuple-element.65), calls=%async_computation.1 | async-start | bytes 3145728 | tf_op jit(solution)/shard_map/all_to_all | solution.py:418
  111.9 22.5 %collective-permute-done.17.refs_5_ = bf16[1024,512]{1,0:T(8,128)(2,1)} collective-permute-done((bf16[1024,512]{1,0:T(8,128)(2,1)S(1)}, bf16[1024,512]{1,0:T(8,128)(2,1)}, u32[]{:S(2)}, u32[]{:S(2)}) %collective-permute-start.17) | collective-permute-done | bytes 1048608 | tf_op jit(solution)/shard_map/ppermute | solution.py:423
  138.1 4.7 %collective-permute-start.25 = (bf16[1024,512]{1,0:T(8,128)(2,1)}, bf16[1024,512]{1,0:T(8,128)(2,1)}, u32[]{:S(2)}, u32[]{:S(2)}) collective-permute-start(bf16[1024,512]{1,0:T(8,128)(2,1)} %collective-permute-done.19.refs_9_), channel_id=1, source_target_pairs={{0,2},{1,3},{2,0},{3,1},{4,6},{5,7},{6,4},{7,5},{8,10},{9,11},{10,... | collective-permute-start | bytes 3145736 | tf_op jit(solution)/shard_map/ppermute | solution.py:423
  143.3 10.2 %all-to-all-done.1.third_ref = bf16[8,128,768]{2,1,0:T(8,128)(2,1)} async-done(((bf16[8,128,768]{2,1,0:T(8,128)(2,1)}), bf16[8,128,768]{2,1,0:T(8,128)(2,1)}, u32[]{:S(2)}, u32[]{:S(2)}) %all-to-all-start.1) | async-done | bytes 1572896 | tf_op jit(solution)/shard_map/all_to_all | solution.py:418
  153.5 12.4 %shard_map.103 = (bf16[8,128,768]{2,1,0:T(8,128)(2,1)}, f32[2,1024,128]{2,1,0:T(8,128)}) custom-call(bf16[8,128,768]{2,1,0:T(8,128)(2,1)} %all-to-all-done.1.third_ref, bf16[1792,1024]{1,0:T(8,128)(2,1)} %teach_ref.3, bf16[1024,1024]{1,0:T(8,128)(2,1)} %bitcast.168, bf16[1024,1024]{1,0:T(8,128)(2,1)} %bitcast.180), custom_call_target="tpu_custom_call" | custom-call | flops 4831838208 | bytes 8912896 | tf_op jit(solution)/shard_map/pallas_call | solution.py:159
  165.9 9.0 %collective-permute-done.24.refs_12_ = bf16[1024,512]{1,0:T(8,128)(2,1)S(1)} collective-permute-done((bf16[1024,512]{1,0:T(8,128)(2,1)}, bf16[1024,512]{1,0:T(8,128)(2,1)S(1)}, u32[]{:S(2)}, u32[]{:S(2)}) %collective-permute-start.24) | collective-permute-done | bytes 1048608 | tf_op jit(solution)/shard_map/ppermute | solution.py:423
  180.9 17.9 %shard_map.104 = (bf16[32,128,1024]{2,1,0:T(8,128)(2,1)}, bf16[8,128,1024]{2,1,0:T(8,128)(2,1)}) custom-call(bf16[1024,512]{1,0:T(8,128)(2,1)} %copy-done.6, bf16[1024,512]{1,0:T(8,128)(2,1)} %copy-done.5, bf16[1024,512]{1,0:T(8,128)(2,1)} %collective-permute-done.14.refs_2_, bf16[1024,512]{1,0:T(8,128)(2,1)} %collective-permute-done.15.refs_3_, ...), custom_call_target="tpu_custom_call" | custom-call | flops 6442450944 | bytes 26214400 | tf_op jit(solution)/shard_map/pallas_call | solution.py:105
  202.2 4.4 all-to-all-start.2
  206.5 23.7 %shard_map.105 = (bf16[16,256,768]{2,1,0:T(8,128)(2,1)}, bf16[32,128,768]{2,1,0:T(8,128)(2,1)}, bf16[8,512,768]{2,1,0:T(8,128)(2,1)}) custom-call(s32[16]{0:T(128)} %iota_xor_fusion.refs_16_.order_ref, bf16[32,128,768]{2,1,0:T(8,128)(2,1)} %get-tuple-element.77.first_ref, bf16[8,128,768]{2,1,0:T(8,128)(2,1)} %copy-done.2, bf16[32,128,128]{2,1,0:T(8,128)(2,1)} %w2_ref.3, ...), custom_call_target="tpu_custom_call" | custom-call | flops 3221225472 | bytes 26738688 | tf_op jit(solution)/shard_map/pallas_call | solution.py:206
  233.2 15.5 %shard_map.106 = (bf16[8,128,1024]{2,1,0:T(8,128)(2,1)}, f32[4,256,256]{2,1,0:T(8,128)}) custom-call(bf16[8,128,1024]{2,1,0:T(8,128)(2,1)} %all-to-all-done.2.third_ref, bf16[1792,1024]{1,0:T(8,128)(2,1)} %teach_ref.3, bf16[1024,1024]{1,0:T(8,128)(2,1)} %bitcast.169, bf16[1024,1024]{1,0:T(8,128)(2,1)} %bitcast.181, f32[2,1024,128]{2,1,0:T(8,128)} %get-tuple-element.80.refs_0_), custom_call_target="tpu_custom_call" | custom-call | flops 6442450944 | bytes 10485760 | tf_op jit(solution)/shard_map/pallas_call | solution.py:159
  248.7 4.0 all-to-all-start.4
  258.0 10.8 %shard_map.107 = (f32[32,128,128]{2,1,0:T(8,128)}, f32[8,512,128]{2,1,0:T(8,128)}) custom-call(s32[2]{0:T(128)} %broadcast_multiply_fusion.2.turn_ref.refs_17_, bf16[32,128,768]{2,1,0:T(8,128)(2,1)} %get-tuple-element.77.first_ref, bf16[32,128,768]{2,1,0:T(8,128)(2,1)} %get-tuple-element.83.slope_ref, bf16[8,512,768]{2,1,0:T(8,128)(2,1)} %get-tuple-element.84.hid_ref, ...), custom_call_target="tpu_custom_call" | custom-call | flops 1610612736 | bytes 20447232 | tf_op jit(solution)/shard_map/pallas_call | solution.py:278
  268.9 9.9 %shard_map.108.refs_19_ = f32[16,256,128]{2,1,0:T(8,128)} custom-call(bf16[768,512]{1,0:T(8,128)(2,1)} %get-tuple-element.107.refs_0_, bf16[768,512]{1,0:T(8,128)(2,1)} %get-tuple-element.106.refs_1_, bf16[768,512]{1,0:T(8,128)(2,1)} %copy-done.13, bf16[768,512]{1,0:T(8,128)(2,1)} %collective-permute-done.1.refs_3_, ...), custom_call_target="tpu_custom_call" | custom-call | flops 3221225472 | bytes 18874368 | tf_op jit(solution)/shard_map/pallas_call | solution.py:330
  282.7 29.9 %shard_map.109 = (bf16[16,256,1024]{2,1,0:T(8,128)(2,1)}, bf16[32,128,1024]{2,1,0:T(8,128)(2,1)}, bf16[8,512,1024]{2,1,0:T(8,128)(2,1)}) custom-call(s32[16]{0:T(128)} %iota_xor_fusion.refs_16_.order_ref, bf16[32,128,1024]{2,1,0:T(8,128)(2,1)} %get-tuple-element.91.first_ref, bf16[8,128,1024]{2,1,0:T(8,128)(2,1)} %copy-done, bf16[32,128,128]{2,1,0:T(8,128)(2,1)} %w2_ref.3, ...), custom_call_target="tpu_custom_call" | custom-call | flops 4294967296 | bytes 35651584 | tf_op jit(solution)/shard_map/pallas_call | solution.py:206
  314.1 12.4 %shard_map.110 = bf16[8,8,2,32,128]{4,3,2,1,0:T(8,128)(2,1)} custom-call(bf16[1024,512]{1,0:T(8,128)(2,1)} %copy-done.6, bf16[1024,512]{1,0:T(8,128)(2,1)} %copy-done.5, bf16[1024,512]{1,0:T(8,128)(2,1)} %collective-permute-done.14.refs_2_, bf16[1024,512]{1,0:T(8,128)(2,1)} %collective-permute-done.15.refs_3_, ...), custom_call_target="tpu_custom_call" | custom-call | flops 4294967296 | bytes 25165824 | tf_op jit(solution)/shard_map/pallas_call | solution.py:330
  332.4 18.5 %shard_map.111 = bf16[32,160,128]{2,1,0:T(8,128)(2,1)} custom-call(s32[2]{0:T(128)} %broadcast_multiply_fusion.2.turn_ref.refs_17_, bf16[32,128,1024]{2,1,0:T(8,128)(2,1)} %get-tuple-element.91.first_ref, bf16[32,128,1024]{2,1,0:T(8,128)(2,1)} %get-tuple-element.97.slope_ref, bf16[8,512,1024]{2,1,0:T(8,128)(2,1)} %get-tuple-element.98.hid_ref, ...), custom_call_target="tpu_custom_call" | custom-call | flops 2147483648 | bytes 27262976 | tf_op jit(solution)/shard_map/pallas_call | solution.py:278
  363.3 10.7 %collective-permute-done.43 = bf16[2,4,160,128]{3,2,1,0:T(8,128)(2,1)} collective-permute-done((bf16[2,4,160,128]{3,2,1,0:T(8,128)(2,1)}, bf16[2,4,160,128]{3,2,1,0:T(8,128)(2,1)}, u32[]{:S(2)}, u32[]{:S(2)}) %collective-permute-start.43) | collective-permute-done | bytes 327712 | tf_op jit(solution)/shard_map/ppermute | solution.py:423
  377.0 3.8 all-to-all-start.5
  399.1 17.0 %collective-permute-start.36 = (bf16[2,8,2,32,128]{4,3,2,1,0:T(8,128)(2,1)S(1)}, bf16[2,8,2,32,128]{4,3,2,1,0:T(8,128)(2,1)S(1)}, u32[]{:S(2)}, u32[]{:S(2)}) collective-permute-start(bf16[2,8,2,32,128]{4,3,2,1,0:T(8,128)(2,1)S(1)} %pad_maximum_fusion.9), channel_id=1, source_target_pairs={{0,8},{8,0},{16,24},{24,16},{1,9},{9,1},{17,25},{25,17},{2,10},{10... | collective-permute-start | bytes 786440 | tf_op jit(solution)/shard_map/ppermute | solution.py:423
  416.1 10.5 %collective-permute-start.42 = (bf16[2,4,160,128]{3,2,1,0:T(8,128)(2,1)S(1)}, bf16[2,4,160,128]{3,2,1,0:T(8,128)(2,1)S(1)}, u32[]{:S(2)}, u32[]{:S(2)}) collective-permute-start(bf16[2,4,160,128]{3,2,1,0:T(8,128)(2,1)S(1)} %pad_maximum_fusion.2), channel_id=1, source_target_pairs={{0,8},{8,0},{16,24},{24,16},{1,9},{9,1},{17,25},{25,17},{2,10},{10... | collective-permute-start | bytes 983048 | tf_op jit(solution)/shard_map/ppermute | solution.py:423
  (224 shorter events, 121.7 us)
Async XLA Ops:
  3.8 53.7 %collective-permute-start.2 = (bf16[768,512]{1,0:T(8,128)(2,1)}, bf16[768,512]{1,0:T(8,128)(2,1)}, u32[]{:S(2)}, u32[]{:S(2)}) collective-permute-start(bf16[768,512]{1,0:T(8,128)(2,1)} %get-tuple-element.107.refs_0_), channel_id=1, source_target_pairs={{0,2},{1,3},{2,0},{3,1},{4,6},{5,7},{6,4},{7,5},{8,10},{9,11},{10,... | collective-permute-start | bytes 2359304 | tf_op jit(solution)/shard_map/ppermute | solution.py:423
  6.2 51.2 %collective-permute-start.1 = (bf16[768,512]{1,0:T(8,128)(2,1)}, bf16[768,512]{1,0:T(8,128)(2,1)}, u32[]{:S(2)}, u32[]{:S(2)}) collective-permute-start(bf16[768,512]{1,0:T(8,128)(2,1)} %get-tuple-element.106.refs_1_), channel_id=1, source_target_pairs={{0,1},{1,0},{2,3},{3,2},{4,5},{5,4},{6,7},{7,6},{8,9},{9,8},{10,11... | collective-permute-start | bytes 2359304 | tf_op jit(solution)/shard_map/ppermute | solution.py:423
  6.5 51.0 %collective-permute-start.3 = (bf16[768,512]{1,0:T(8,128)(2,1)}, bf16[768,512]{1,0:T(8,128)(2,1)}, u32[]{:S(2)}, u32[]{:S(2)}) collective-permute-start(bf16[768,512]{1,0:T(8,128)(2,1)} %get-tuple-element.106.refs_1_), channel_id=1, source_target_pairs={{0,2},{1,3},{2,0},{3,1},{4,6},{5,7},{6,4},{7,5},{8,10},{9,11},{10,... | collective-permute-start | bytes 2359304 | tf_op jit(solution)/shard_map/ppermute | solution.py:423
  6.8 50.7 %collective-permute-start.4 = (bf16[768,512]{1,0:T(8,128)(2,1)}, bf16[768,512]{1,0:T(8,128)(2,1)}, u32[]{:S(2)}, u32[]{:S(2)}) collective-permute-start(bf16[768,512]{1,0:T(8,128)(2,1)} %get-tuple-element.107.refs_0_), channel_id=1, source_target_pairs={{0,4},{1,5},{2,6},{3,7},{4,0},{5,1},{6,2},{7,3},{8,12},{9,13},{10,... | collective-permute-start | bytes 2359304 | tf_op jit(solution)/shard_map/ppermute | solution.py:423
  10.3 43.9 %all-to-all-start = ((bf16[8,8,2,32,128]{4,3,2,1,0:T(8,128)(2,1)}), bf16[8,8,2,32,128]{4,3,2,1,0:T(8,128)(2,1)}, u32[]{:S(2)}, u32[]{:S(2)}) async-start(bf16[8,8,2,32,128]{4,3,2,1,0:T(8,128)(2,1)} %copy.32), calls=%async_computation | async-start | bytes 2097152 | tf_op jit(solution)/shard_map/all_to_all | solution.py:418
  15.1 42.3 %collective-permute-start.5 = (bf16[768,512]{1,0:T(8,128)(2,1)}, bf16[768,512]{1,0:T(8,128)(2,1)}, u32[]{:S(2)}, u32[]{:S(2)}) collective-permute-start(bf16[768,512]{1,0:T(8,128)(2,1)} %get-tuple-element.106.refs_1_), channel_id=1, source_target_pairs={{0,4},{1,5},{2,6},{3,7},{4,0},{5,1},{6,2},{7,3},{8,12},{9,13},{10,... | collective-permute-start | bytes 2359304 | tf_op jit(solution)/shard_map/ppermute | solution.py:423
  85.8 26.1 %collective-permute-start.16 = (bf16[1024,512]{1,0:T(8,128)(2,1)S(1)}, bf16[1024,512]{1,0:T(8,128)(2,1)}, u32[]{:S(2)}, u32[]{:S(2)}) collective-permute-start(bf16[1024,512]{1,0:T(8,128)(2,1)S(1)} %get-tuple-element.105.refs_0_), channel_id=1, source_target_pairs={{0,2},{1,3},{2,0},{3,1},{4,6},{5,7},{6,4},{7,5},{8,10},{9,11},{10,... | collective-permute-start | bytes 3145736 | tf_op jit(solution)/shard_map/ppermute | solution.py:423
  86.6 47.8 %collective-permute-start.17 = (bf16[1024,512]{1,0:T(8,128)(2,1)S(1)}, bf16[1024,512]{1,0:T(8,128)(2,1)}, u32[]{:S(2)}, u32[]{:S(2)}) collective-permute-start(bf16[1024,512]{1,0:T(8,128)(2,1)S(1)} %get-tuple-element.104.refs_1_), channel_id=1, source_target_pairs={{0,2},{1,3},{2,0},{3,1},{4,6},{5,7},{6,4},{7,5},{8,10},{9,11},{10,... | collective-permute-start | bytes 3145736 | tf_op jit(solution)/shard_map/ppermute | solution.py:423
  88.1 46.3 %collective-permute-start.18 = (bf16[1024,512]{1,0:T(8,128)(2,1)S(1)}, bf16[1024,512]{1,0:T(8,128)(2,1)}, u32[]{:S(2)}, u32[]{:S(2)}) collective-permute-start(bf16[1024,512]{1,0:T(8,128)(2,1)S(1)} %get-tuple-element.105.refs_0_), channel_id=1, source_target_pairs={{0,4},{1,5},{2,6},{3,7},{4,0},{5,1},{6,2},{7,3},{8,12},{9,13},{10,... | collective-permute-start | bytes 3145736 | tf_op jit(solution)/shard_map/ppermute | solution.py:423
  89.5 47.2 %collective-permute-start.19 = (bf16[1024,512]{1,0:T(8,128)(2,1)S(1)}, bf16[1024,512]{1,0:T(8,128)(2,1)}, u32[]{:S(2)}, u32[]{:S(2)}) collective-permute-start(bf16[1024,512]{1,0:T(8,128)(2,1)S(1)} %get-tuple-element.104.refs_1_), channel_id=1, source_target_pairs={{0,4},{1,5},{2,6},{3,7},{4,0},{5,1},{6,2},{7,3},{8,12},{9,13},{10,... | collective-permute-start | bytes 3145736 | tf_op jit(solution)/shard_map/ppermute | solution.py:423
  104.7 48.8 %all-to-all-start.1 = ((bf16[8,128,768]{2,1,0:T(8,128)(2,1)}), bf16[8,128,768]{2,1,0:T(8,128)(2,1)}, u32[]{:S(2)}, u32[]{:S(2)}) async-start(bf16[8,128,768]{2,1,0:T(8,128)(2,1)} %get-tuple-element.65), calls=%async_computation.1 | async-start | bytes 3145728 | tf_op jit(solution)/shard_map/all_to_all | solution.py:418
  136.7 38.3 %collective-permute-start.24 = (bf16[1024,512]{1,0:T(8,128)(2,1)}, bf16[1024,512]{1,0:T(8,128)(2,1)S(1)}, u32[]{:S(2)}, u32[]{:S(2)}) collective-permute-start(bf16[1024,512]{1,0:T(8,128)(2,1)} %collective-permute-done.16.refs_4_), channel_id=1, source_target_pairs={{0,4},{1,5},{2,6},{3,7},{4,0},{5,1},{6,2},{7,3},{8,12},{9,13},{10,... | collective-permute-start | bytes 3145736 | tf_op jit(solution)/shard_map/ppermute | solution.py:423
  138.1 36.9 %collective-permute-start.25 = (bf16[1024,512]{1,0:T(8,128)(2,1)}, bf16[1024,512]{1,0:T(8,128)(2,1)}, u32[]{:S(2)}, u32[]{:S(2)}) collective-permute-start(bf16[1024,512]{1,0:T(8,128)(2,1)} %collective-permute-done.19.refs_9_), channel_id=1, source_target_pairs={{0,2},{1,3},{2,0},{3,1},{4,6},{5,7},{6,4},{7,5},{8,10},{9,11},{10,... | collective-permute-start | bytes 3145736 | tf_op jit(solution)/shard_map/ppermute | solution.py:423
  142.8 32.6 %collective-permute-start.20 = (bf16[1024,512]{1,0:T(8,128)(2,1)}, bf16[1024,512]{1,0:T(8,128)(2,1)S(1)}, u32[]{:S(2)}, u32[]{:S(2)}) collective-permute-start(bf16[1024,512]{1,0:T(8,128)(2,1)} %collective-permute-done.16.refs_4_), channel_id=1, source_target_pairs={{0,1},{1,0},{2,3},{3,2},{4,5},{5,4},{6,7},{7,6},{8,9},{9,8},{10,11... | collective-permute-start | bytes 3145736 | tf_op jit(solution)/shard_map/ppermute | solution.py:423
  142.8 37.3 %collective-permute-start.23 = (bf16[1024,512]{1,0:T(8,128)(2,1)}, bf16[1024,512]{1,0:T(8,128)(2,1)}, u32[]{:S(2)}, u32[]{:S(2)}) collective-permute-start(bf16[1024,512]{1,0:T(8,128)(2,1)} %collective-permute-done.19.refs_9_), channel_id=1, source_target_pairs={{0,1},{1,0},{2,3},{3,2},{4,5},{5,4},{6,7},{7,6},{8,9},{9,8},{10,11... | collective-permute-start | bytes 3145736 | tf_op jit(solution)/shard_map/ppermute | solution.py:423
  143.3 36.7 %collective-permute-start.21 = (bf16[1024,512]{1,0:T(8,128)(2,1)}, bf16[1024,512]{1,0:T(8,128)(2,1)}, u32[]{:S(2)}, u32[]{:S(2)}) collective-permute-start(bf16[1024,512]{1,0:T(8,128)(2,1)} %collective-permute-done.17.refs_5_), channel_id=1, source_target_pairs={{0,1},{1,0},{2,3},{3,2},{4,5},{5,4},{6,7},{7,6},{8,9},{9,8},{10,11... | collective-permute-start | bytes 3145736 | tf_op jit(solution)/shard_map/ppermute | solution.py:423
  202.2 31.0 %all-to-all-start.2 = ((bf16[8,128,1024]{2,1,0:T(8,128)(2,1)}), bf16[8,128,1024]{2,1,0:T(8,128)(2,1)}, u32[]{:S(2)}, u32[]{:S(2)}) async-start(bf16[8,128,1024]{2,1,0:T(8,128)(2,1)} %get-tuple-element.75), calls=%async_computation.2 | async-start | bytes 4194304 | tf_op jit(solution)/shard_map/all_to_all | solution.py:418
  248.7 32.7 %all-to-all-start.4 = ((bf16[8,128,1024]{2,1,0:T(8,128)(2,1)}), bf16[8,128,1024]{2,1,0:T(8,128)(2,1)S(1)}, u32[]{:S(2)}, u32[]{:S(2)}) async-start(bf16[8,128,1024]{2,1,0:T(8,128)(2,1)} %get-tuple-element.81), calls=%async_computation.4 | async-start | bytes 4194304 | tf_op jit(solution)/shard_map/all_to_all | solution.py:418
  278.8 33.8 %collective-permute-start.29 = (bf16[512,128]{1,0:T(8,128)(2,1)S(1)}, bf16[512,128]{1,0:T(8,128)(2,1)S(1)}, u32[]{:S(2)}, u32[]{:S(2)}) collective-permute-start(bf16[512,128]{1,0:T(8,128)(2,1)S(1)} %get-tuple-element.114), channel_id=1, source_target_pairs={{0,24},{8,16},{16,8},{24,0},{1,25},{9,17},{17,9},{25,1},{2,26},{10... | collective-permute-start | bytes 393224 | tf_op jit(solution)/shard_map/ppermute | solution.py:423
  330.3 27.3 %collective-permute-start.47 = (bf16[2,512,128]{2,1,0:T(8,128)(2,1)S(1)}, bf16[2,512,128]{2,1,0:T(8,128)(2,1)S(1)}, u32[]{:S(2)}, u32[]{:S(2)}) collective-permute-start(bf16[2,512,128]{2,1,0:T(8,128)(2,1)S(1)} %pad_maximum_fusion.7), channel_id=1, source_target_pairs={{0,8},{8,0},{16,24},{24,16},{1,9},{9,1},{17,25},{25,17},{2,10},{10... | collective-permute-start | bytes 786440 | tf_op jit(solution)/shard_map/ppermute | solution.py:423
  354.4 26.4 %collective-permute-start.39 = (bf16[2,4,160,128]{3,2,1,0:T(8,128)(2,1)}, bf16[2,4,160,128]{3,2,1,0:T(8,128)(2,1)}, u32[]{:S(2)}, u32[]{:S(2)}) collective-permute-start(bf16[2,4,160,128]{3,2,1,0:T(8,128)(2,1)} %pad_maximum_fusion.1), channel_id=1, source_target_pairs={{0,8},{8,0},{16,24},{24,16},{1,9},{9,1},{17,25},{25,17},{2,10},{10... | collective-permute-start | bytes 983048 | tf_op jit(solution)/shard_map/ppermute | solution.py:423
  390.7 35.9 %collective-permute-start.46 = (bf16[2,4,160,128]{3,2,1,0:T(8,128)(2,1)S(1)}, bf16[2,4,160,128]{3,2,1,0:T(8,128)(2,1)S(1)}, u32[]{:S(2)}, u32[]{:S(2)}) collective-permute-start(bf16[2,4,160,128]{3,2,1,0:T(8,128)(2,1)S(1)} %pad_maximum_fusion.4), channel_id=1, source_target_pairs={{0,24},{8,16},{16,8},{24,0},{1,25},{9,17},{17,9},{25,1},{2,26},{10... | collective-permute-start | bytes 983048 | tf_op jit(solution)/shard_map/ppermute | solution.py:423
  396.6 30.7 %collective-permute-start.38 = (bf16[2,8,2,32,128]{4,3,2,1,0:T(8,128)(2,1)S(1)}, bf16[2,8,2,32,128]{4,3,2,1,0:T(8,128)(2,1)S(1)}, u32[]{:S(2)}, u32[]{:S(2)}) collective-permute-start(bf16[2,8,2,32,128]{4,3,2,1,0:T(8,128)(2,1)S(1)} %pad_maximum_fusion.10), channel_id=1, source_target_pairs={{0,24},{8,16},{16,8},{24,0},{1,25},{9,17},{17,9},{25,1},{2,26},{10... | collective-permute-start | bytes 786440 | tf_op jit(solution)/shard_map/ppermute | solution.py:423
  399.1 29.0 %collective-permute-start.36 = (bf16[2,8,2,32,128]{4,3,2,1,0:T(8,128)(2,1)S(1)}, bf16[2,8,2,32,128]{4,3,2,1,0:T(8,128)(2,1)S(1)}, u32[]{:S(2)}, u32[]{:S(2)}) collective-permute-start(bf16[2,8,2,32,128]{4,3,2,1,0:T(8,128)(2,1)S(1)} %pad_maximum_fusion.9), channel_id=1, source_target_pairs={{0,8},{8,0},{16,24},{24,16},{1,9},{9,1},{17,25},{25,17},{2,10},{10... | collective-permute-start | bytes 786440 | tf_op jit(solution)/shard_map/ppermute | solution.py:423
  (64 other events, 815.2 us)
